TPU v7x, 32 devices: a whole 2x2x4 slice. The times are simulated.
32 devices in a mesh: member: 4 (over y, core), lat: 2 (over x), lon: 4 (over z).
Axes of the slice: x: 2, y: 2, z: 4, core: 2. Of those that a mesh axis runs over, the one named last changes fastest.
Arguments:
- fields: bfloat16 [12, 32, 32, 256], P('member', 'lat', 'lon'), may hold values from -6 to 6
- land_mask: int32 [32, 32], P('lat', 'lon'), may hold values 0 or 1
- offsets: int32 [2], replicated, may hold values from 1 to 7
- land_embed: float32 [256], replicated, may hold values from -5 to 5
- win_qkv: bfloat16 [256, 768], replicated, may hold values from -16 to 16, as said below
- win_out: bfloat16 [256, 256], replicated, may hold values from -0.375 to 0.375
- win_up: bfloat16 [256, 1024], replicated, may hold values from -0.375 to 0.375
- win_down: bfloat16 [1024, 256], replicated, may hold values from -0.1875 to 0.1875
- mem_qkv: bfloat16 [256, 768], replicated, may hold values from -16 to 16, as said below
- mem_out: bfloat16 [256, 256], replicated, may hold values from -0.375 to 0.375
- shift_qkv: bfloat16 [256, 768], replicated, may hold values from -16 to 16, as said below
- shift_out: bfloat16 [256, 256], replicated, may hold values from -0.375 to 0.375
- shift_up: bfloat16 [256, 1024], replicated, may hold values from -0.375 to 0.375
- shift_down: bfloat16 [1024, 256], replicated, may hold values from -0.1875 to 0.1875
Outputs:
- updated: bfloat16 [12, 32, 32, 256], P('member', 'lat', 'lon')
Inputs may be any that keep to these rules, and one draw needn't show every extreme that they name: `win_qkv`: query, key and value projection: columns 0 to 255 are queries, then keys, then values, each in 4 heads of 64. `mem_qkv`: laid out as win_qkv. `shift_qkv`: laid out as win_qkv.
All inputs are finite; a program needn't handle non-finite values. No bound on the sum of `land_mask` on one device may be relied on, other than what follows from the above.
Results may differ from a plain program's by a relative error of at most 0.013.
Values may be sent and summed in bfloat16 or wider, within the bound.
No kernel may reach another device: no remote copies, remote signals or barrier semaphores. Data moves between devices by JAX's collectives and lax.ppermute only.
A program may use at most 64 MiB of HBM per device.

v0:
```python
import jax
import jax.numpy as jnp
from jax import lax
from jax.sharding import PartitionSpec as P

HEADS = 4
WIN = 8


epsilon = 1e-05


def with_halo(block, sides, width):
    for axis, dim in sides:
        count = lax.axis_size(axis)
        forward = [(i, i + 1) for i in range(count - 1)]
        forward.append((count - 1, 0))
        backward = [(target, source) for source, target in forward]
        low = lax.ppermute(
            lax.slice_in_dim(block, block.shape[dim] - width, None, axis=dim), axis, forward
        )
        high = lax.ppermute(lax.slice_in_dim(block, 0, width, axis=dim), axis, backward)
        block = jnp.concatenate([low, block, high], axis=dim)
    return block


def normalize(stream):
    average = jnp.mean(stream, axis=-1, keepdims=True)
    centered = stream - average
    spread = jnp.mean(centered * centered, axis=-1, keepdims=True)
    return (centered * lax.rsqrt(spread + epsilon)).astype(jnp.bfloat16)


def project(inputs, matrix):
    flattened = inputs.reshape(-1, inputs.shape[-1])
    result = jnp.dot(flattened, matrix, preferred_element_type=jnp.float32)
    return result.reshape(inputs.shape[:-1] + (matrix.shape[1],))


def to_windows(tensor):
    height, breadth, channels = tensor.shape
    tensor = tensor.reshape(height // WIN, WIN, breadth // WIN, WIN, channels)
    return tensor.transpose(0, 2, 1, 3, 4).reshape(
        height // WIN, breadth // WIN, WIN * WIN, channels
    )


def from_windows(tensor, height, breadth):
    channels = tensor.shape[-1]
    tensor = tensor.reshape(height // WIN, breadth // WIN, WIN, WIN, channels).transpose(
        0, 2, 1, 3, 4
    )
    return tensor.reshape(height, breadth, channels)


def plain_windows(qkv_rows):
    height, breadth, triple = qkv_rows.shape
    channels = triple // 3
    head_size = channels // HEADS
    blocks = to_windows(qkv_rows)
    split_heads = blocks.reshape(blocks.shape[:3] + (3, HEADS, head_size))
    scores = jnp.einsum(
        "abqhe,abkhe->abhqk",
        split_heads[:, :, :, 0],
        split_heads[:, :, :, 1],
        preferred_element_type=jnp.float32,
    ) * head_size ** (-0.5)
    weights = jax.nn.softmax(scores, axis=-1).astype(jnp.bfloat16)
    result = jnp.einsum(
        "abhqk,abkhe->abqhe", weights, split_heads[:, :, :, 2], preferred_element_type=jnp.float32
    ).astype(jnp.bfloat16)
    return from_windows(result.reshape(blocks.shape[:3] + (channels,)), height, breadth)


def feed_forward(stream, w_up, w_down):
    hidden = jax.nn.gelu(project(normalize(stream), w_up), approximate=False).astype(jnp.bfloat16)
    return stream + project(hidden, w_down)


def member_attention(qkv_rows):
    members, ignored, amount, triple = qkv_rows.shape
    channels = triple // 3
    head_size = channels // HEADS
    split_heads = qkv_rows.reshape(members, amount, 3, HEADS, head_size)
    scores = jnp.einsum(
        "mthe,nthe->thmn",
        split_heads[:, :, 0],
        split_heads[:, :, 1],
        preferred_element_type=jnp.float32,
    ) * head_size ** (-0.5)
    weights = jax.nn.softmax(scores, axis=-1).astype(jnp.bfloat16)
    result = jnp.einsum(
        "thmn,nthe->mthe", weights, split_heads[:, :, 2], preferred_element_type=jnp.float32
    ).astype(jnp.bfloat16)
    return result.reshape(members, 1, amount, channels)


def shifted_attention(queries, borders, offsets, lat_first, lon_first, lat_total, lon_total):
    members, height, breadth, channels = queries.shape
    margin = (borders.shape[1] - height) // 2
    head_size = channels // HEADS
    q_rows = lat_first + jnp.arange(height, dtype=jnp.int32)
    q_cols = lon_first + jnp.arange(breadth, dtype=jnp.int32)
    k_rows = lat_first - margin + jnp.arange(height + 2 * margin, dtype=jnp.int32)
    k_cols = (lon_first - margin + jnp.arange(breadth + 2 * margin, dtype=jnp.int32)) % lon_total
    q_lat = jnp.floor_divide(q_rows - offsets[0], WIN)
    inside = (k_rows >= 0) & (k_rows < lat_total)
    k_lat = jnp.where(inside, jnp.floor_divide(k_rows - offsets[0], WIN), -1000)
    q_lon = jnp.floor_divide((q_cols - offsets[1]) % lon_total, WIN)
    k_lon = jnp.floor_divide((k_cols - offsets[1]) % lon_total, WIN)
    allowed = (q_lat[:, None, None, None] == k_lat[None, None, :, None]) & (
        q_lon[None, :, None, None] == k_lon[None, None, None, :]
    )
    allowed = allowed.reshape(height * breadth, -1)
    query_heads = queries.reshape(members, height * breadth, HEADS, head_size)
    key_heads = borders[..., :channels].reshape(members, -1, HEADS, head_size)
    value_heads = borders[..., channels:].reshape(members, -1, HEADS, head_size)

    def attend_member(operands):
        query_part, key_part, value_part = operands
        scores = jnp.einsum(
            "qhe,khe->hqk", query_part, key_part, preferred_element_type=jnp.float32
        ) * head_size ** (-0.5)
        scores = jnp.where(allowed[None], scores, -1e30)
        weights = jax.nn.softmax(scores, axis=-1).astype(jnp.bfloat16)
        return jnp.einsum(
            "hqk,khe->qhe", weights, value_part, preferred_element_type=jnp.float32
        ).astype(jnp.bfloat16)

    result = lax.map(attend_member, (query_heads, key_heads, value_heads))
    return result.reshape(members, height, breadth, channels)


def per_device(
    fields,
    land_mask,
    offsets,
    land_embed,
    win_qkv,
    win_out,
    win_up,
    win_down,
    mem_qkv,
    mem_out,
    shift_qkv,
    shift_out,
    shift_up,
    shift_down,
):
    members, height, breadth, channels = fields.shape
    stream = (
        fields.astype(jnp.float32)
        + land_mask.astype(jnp.float32)[None, :, :, None] * land_embed[None, None, None, :]
    )
    qkv_rows = project(normalize(stream), win_qkv).astype(jnp.bfloat16)
    attended = jax.vmap(plain_windows)(qkv_rows)
    stream = stream + project(attended, win_out)
    stream = feed_forward(stream, win_up, win_down)
    groups = lax.axis_size("member")
    amount = height * breadth // groups
    normed = normalize(stream).reshape(members, groups, amount, channels)
    projected = project(normed, mem_qkv).astype(jnp.bfloat16)
    mixed = member_attention(
        lax.all_to_all(projected, "member", split_axis=1, concat_axis=0, tiled=True)
    )
    returned = lax.all_to_all(mixed, "member", split_axis=0, concat_axis=1, tiled=True)
    stream = stream + project(returned.reshape(members, height, breadth, channels), mem_out)
    normed_late = normalize(stream)
    rim = with_halo(normed_late, (("lat", 1), ("lon", 2)), WIN - 1)
    borders = project(rim, shift_qkv[:, channels:]).astype(jnp.bfloat16)
    queries = project(normed_late, shift_qkv[:, :channels]).astype(jnp.bfloat16)
    lat_first = lax.axis_index("lat") * height
    lon_first = lax.axis_index("lon") * breadth
    attended = shifted_attention(
        queries,
        borders,
        offsets,
        lat_first,
        lon_first,
        height * lax.axis_size("lat"),
        breadth * lax.axis_size("lon"),
    )
    stream = stream + project(attended, shift_out)
    stream = feed_forward(stream, shift_up, shift_down)
    return stream.astype(jnp.bfloat16)


def solution(mesh):
    return jax.shard_map(
        per_device,
        mesh=mesh,
        in_specs=(
            P("member", "lat", "lon", None),
            P("lat", "lon"),
            P(),
            P(),
            P(),
            P(),
            P(),
            P(),
            P(),
            P(),
            P(),
            P(),
            P(),
            P(),
        ),
        out_specs=P("member", "lat", "lon", None),
        check_vma=False,
    )
```

profile of v0, /device:TPU:0, one launch (start us, length us, event | category | flops | bytes accessed | tf_op | source)
XLA Modules:
  0.0 116.2 jit_solution(18362728204416238010)
XLA Ops:
  2.7 1.2 multiply_reduce_fusion.4
  3.8 1.5 %convolution_convert_fusion.3 = bf16[3,16,8,768]{3,2,1,0:T(8,128)(2,1)S(1)} fusion(bf16[256,768]{1,0:T(8,128)(2,1)} %param.20, bf16[3,16,8,256]{3,2,1,0:T(8,128)(2,1)} %param.16, f32[3,16,8]{2,1,0:T(8,128)S(1)} %add_rsqrt_fusion.4, f32[3,16,8]{2,1,0:T(8,128)S(1)} %broadcast_multiply_fusion.5, f32[16,8,256]{2,1,0:T(8,128)S(1)} %broadcast_multiply_fusion), kind=kOutput, calls=%fused_computation.79 | convolution fusion | flops 151781376 | bytes 1313792 | tf_op jit(solution)/shard_map/dot_general | solution.py:36
  10.2 4.1 %fusion.194 = (f32[3,16,8]{2,1,0:T(8,128)S(1)}, f32[3,16,8,256]{3,2,1,0:T(8,128)S(1)}) fusion(f32[3,16,8,256]{3,2,1,0:T(8,128)S(1)} %get-tuple-element.110, bf16[1024,256]{1,0:T(8,128)(2,1)S(1)} %copy-done.10, f32[3,16,8,1024]{3,2,1,0:T(8,128)S(1)} %get-tuple-element.111, u16[3,8,1024]{2,1,0:T(8,128)(2,1)S(1)} %get-tuple-element.80, ...), kind=kOutput, calls=%fused_computation.267 | convolution fusion | flops 229047936 | bytes 2983424 | tf_op jit(solution)/shard_map/dot_general | solution.py:36
  16.0 4.2 %all-to-all-start = ((bf16[3,4,32,768]{3,2,0,1:T(8,128)(2,1)}), bf16[3,4,32,768]{3,2,0,1:T(8,128)(2,1)S(1)}, u32[]{:S(2)}, u32[]{:S(2)}) async-start(bf16[3,4,32,768]{3,2,0,1:T(8,128)(2,1)} %copy.52), calls=%async_computation | async-start | bytes 1179648 | tf_op jit(solution)/shard_map/all_to_all | solution.py:164
  22.1 7.6 %all-to-all-done = bf16[3,4,32,768]{3,2,0,1:T(8,128)(2,1)S(1)} async-done(((bf16[3,4,32,768]{3,2,0,1:T(8,128)(2,1)}), bf16[3,4,32,768]{3,2,0,1:T(8,128)(2,1)S(1)}, u32[]{:S(2)}, u32[]{:S(2)}) %all-to-all-start) | async-done | bytes 589856 | tf_op jit(solution)/shard_map/all_to_all | solution.py:164
  33.5 3.4 %all-to-all-start.1 = ((bf16[12,1,32,256]{3,2,1,0:T(8,128)(2,1)}), bf16[12,1,32,256]{3,2,1,0:T(8,128)(2,1)S(1)}, u32[]{:S(2)}, u32[]{:S(2)}) async-start(bf16[12,1,32,256]{3,2,1,0:T(8,128)(2,1)} %bitcast.22), calls=%async_computation.1 | async-start | bytes 393216 | tf_op jit(solution)/shard_map/all_to_all | solution.py:166
  37.5 4.6 %all-to-all-done.1 = bf16[12,1,32,256]{3,2,1,0:T(8,128)(2,1)S(1)} async-done(((bf16[12,1,32,256]{3,2,1,0:T(8,128)(2,1)}), bf16[12,1,32,256]{3,2,1,0:T(8,128)(2,1)S(1)}, u32[]{:S(2)}, u32[]{:S(2)}) %all-to-all-start.1) | async-done | bytes 196640 | tf_op jit(solution)/shard_map/all_to_all | solution.py:166
  43.0 2.2 %collective-permute-start = (bf16[3,7,8,256]{3,2,1,0:T(8,128)(2,1)S(1)}, bf16[3,7,8,256]{3,2,1,0:T(8,128)(2,1)S(1)}, u32[]{:S(2)}, u32[]{:S(2)}) collective-permute-start(bf16[3,7,8,256]{3,2,1,0:T(8,128)(2,1)S(1)} %get-tuple-element.105), channel_id=1, source_target_pairs={{0,4},{4,0},{1,5},{5,1},{2,6},{6,2},{3,7},{7,3},{8,12},{12,8},{9,1... | collective-permute-start | bytes 258056 | tf_op jit(solution)/shard_map/ppermute | solution.py:19
  45.9 2.4 %collective-permute-done = bf16[3,7,8,256]{3,2,1,0:T(8,128)(2,1)S(1)} collective-permute-done((bf16[3,7,8,256]{3,2,1,0:T(8,128)(2,1)S(1)}, bf16[3,7,8,256]{3,2,1,0:T(8,128)(2,1)S(1)}, u32[]{:S(2)}, u32[]{:S(2)}) %collective-permute-start) | collective-permute-done | bytes 86048 | tf_op jit(solution)/shard_map/ppermute | solution.py:19
  48.3 1.4 %collective-permute-done.1 = bf16[3,7,8,256]{3,2,1,0:T(8,128)(2,1)S(1)} collective-permute-done((bf16[3,7,8,256]{3,2,1,0:T(8,128)(2,1)S(1)}, bf16[3,7,8,256]{3,2,1,0:T(8,128)(2,1)S(1)}, u32[]{:S(2)}, u32[]{:S(2)}) %collective-permute-start.1) | collective-permute-done | bytes 86048 | tf_op jit(solution)/shard_map/ppermute | solution.py:22
  50.6 1.8 %collective-permute-start.2 = (bf16[3,30,7,256]{3,2,1,0:T(8,128)(2,1)}, bf16[3,30,7,256]{3,2,1,0:T(8,128)(2,1)S(1)}, u32[]{:S(2)}, u32[]{:S(2)}) collective-permute-start(bf16[3,30,7,256]{3,2,1,0:T(8,128)(2,1)} %get-tuple-element.103), channel_id=1, source_target_pairs={{0,1},{1,2},{2,3},{3,0},{4,5},{5,6},{6,7},{7,4},{8,9},{9,10},{10,1... | collective-permute-start | bytes 967688 | tf_op jit(solution)/shard_map/ppermute | solution.py:19
  52.4 2.0 %collective-permute-start.3 = (bf16[3,30,7,256]{3,2,1,0:T(8,128)(2,1)S(1)}, bf16[3,30,7,256]{3,2,1,0:T(8,128)(2,1)S(1)}, u32[]{:S(2)}, u32[]{:S(2)}) collective-permute-start(bf16[3,30,7,256]{3,2,1,0:T(8,128)(2,1)S(1)} %get-tuple-element.104), channel_id=1, source_target_pairs={{1,0},{2,1},{3,2},{0,3},{5,4},{6,5},{7,6},{4,7},{9,8},{10,9},{11,1... | collective-permute-start | bytes 967688 | tf_op jit(solution)/shard_map/ppermute | solution.py:22
  55.8 8.4 %collective-permute-done.2 = bf16[3,30,7,256]{3,2,1,0:T(8,128)(2,1)S(1)} collective-permute-done((bf16[3,30,7,256]{3,2,1,0:T(8,128)(2,1)}, bf16[3,30,7,256]{3,2,1,0:T(8,128)(2,1)S(1)}, u32[]{:S(2)}, u32[]{:S(2)}) %collective-permute-start.2) | collective-permute-done | bytes 322592 | tf_op jit(solution)/shard_map/ppermute | solution.py:19
  64.2 5.4 %collective-permute-done.3 = bf16[3,30,7,256]{3,2,1,0:T(8,128)(2,1)S(1)} collective-permute-done((bf16[3,30,7,256]{3,2,1,0:T(8,128)(2,1)S(1)}, bf16[3,30,7,256]{3,2,1,0:T(8,128)(2,1)S(1)}, u32[]{:S(2)}, u32[]{:S(2)}) %collective-permute-start.3) | collective-permute-done | bytes 322592 | tf_op jit(solution)/shard_map/ppermute | solution.py:22
  70.9 1.2 %fusion.186 = (bf16[3,30,22,256]{3,1,2,0:T(8,128)(2,1)}, bf16[3,30,22,256]{3,1,2,0:T(8,128)(2,1)S(1)}) fusion(bf16[3,30,22,512]{3,1,2,0:T(8,128)(2,1)S(1)} %convolution_convert_fusion.1), kind=kLoop, calls=%fused_computation.259 | loop fusion | bytes 4055040 | tf_op jit(solution)/shard_map/slice | solution.py:116
  72.1 1.6 %copy.61 = bf16[3,30,22,256]{3,2,1,0:T(8,128)(2,1)} copy(bf16[3,30,22,256]{3,1,2,0:T(8,128)(2,1)S(1)} %get-tuple-element.96) | data formatting | bytes 2027520 | tf_op jit(solution)/shard_map/slice | solution.py:117
  73.6 3.3 %reshape.355 = bf16[3,660,4,64]{3,2,1,0:T(4,128)(2,1)S(1)} reshape(bf16[3,30,22,256]{3,2,1,0:T(8,128)(2,1)} %copy.61) | data formatting | bytes 2027520 | tf_op jit(solution)/shard_map/reshape | solution.py:117
  77.0 3.7 %copy.63 = bf16[3,660,4,64]{1,3,2,0:T(8,128)(2,1)} copy(bf16[3,660,4,64]{3,2,1,0:T(4,128)(2,1)S(1)} %reshape.355) | data formatting | bytes 2027520
  80.7 2.8 %copy.62 = bf16[3,30,22,256]{3,2,1,0:T(8,128)(2,1)} copy(bf16[3,30,22,256]{3,1,2,0:T(8,128)(2,1)} %get-tuple-element.95) | data formatting | bytes 2027520 | tf_op jit(solution)/shard_map/slice | solution.py:116
  83.5 3.3 %reshape.357 = bf16[3,660,4,64]{3,2,1,0:T(4,128)(2,1)S(1)} reshape(bf16[3,30,22,256]{3,2,1,0:T(8,128)(2,1)} %copy.62) | data formatting | bytes 2027520 | tf_op jit(solution)/shard_map/reshape | solution.py:116
  86.9 3.8 %copy.65 = bf16[3,660,4,64]{1,3,2,0:T(8,128)(2,1)} copy(bf16[3,660,4,64]{3,2,1,0:T(4,128)(2,1)S(1)} %reshape.357) | data formatting | bytes 2027520
  90.7 18.9 %while.11 = (s32[]{:T(128)}, bf16[3,128,4,64]{1,3,2,0:T(8,128)(2,1)S(1)}, bf16[3,660,4,64]{1,3,2,0:T(8,128)(2,1)}, bf16[3,128,4,64]{1,3,2,0:T(8,128)(2,1)S(1)}, ...) while((s32[]{:T(128)}, ...), condition=%wide.region_15.16_spmd.clone, body=%wide.region_12.15_spmd.clone.sunk | while | flops 132921632 | bytes 1976549 | solution.py:130
  91.0 1.8 %broadcast_in_dim.85 = pred[128,660]{1,0:T(8,128)(4,1)S(1)} reshape(pred[16,8,30,22]{3,2,1,0:T(8,128)(4,1)S(1)} %broadcast_and_fusion.2) | data formatting | bytes 168960 | tf_op jit(solution)/shard_map/while/body/eval_jaxpr/jit(_where)/broadcast_in_dim | solution.py:124
  93.0 1.9 %fusion.216 = f32[4,128]{1,0:T(4,128)S(1)} fusion(pred[128,660]{0,1:T(8,128)(4,1)S(1)} %copy.119, bf16[3,660,4,64]{1,3,2,0:T(8,128)(2,1)} %get-tuple-element.184, s32[]{:T(128)} %get-tuple-element.172, bf16[3,128,4,64]{1,3,2,0:T(8,128)(2,1)S(1)} %get-tuple-element.183), kind=kOutput, calls=%fused_computation.258.clone.1 | convolution fusion | flops 44606100 | bytes 546816 | tf_op jit(solution)/shard_map/while/body/eval_jaxpr/sub | solution.py:125
  94.9 2.1 %fusion.217 = bf16[3,128,4,64]{1,3,2,0:T(8,128)(2,1)S(1)} fusion(bf16[3,128,4,64]{1,3,2,0:T(8,128)(2,1)S(1)} %get-tuple-element.173, s32[]{:T(128)} %get-tuple-element.172, f32[4,128]{1,0:T(4,128)S(1)} %fusion.216, bf16[3,660,4,64]{1,3,2,0:T(8,128)(2,1)} %get-tuple-element.182, pred[128,660]{0,1:T(8,128)(4,1)S(1)} %copy.119, ...), kind=kOutput, calls=%fused_computation.9.clone.1 | convolution fusion | flops 88231056 | bytes 1006592 | tf_op jit(solution)/shard_map/while/body/eval_jaxpr/hqk,khe->qhe/dot_general | solution.py:126
  97.3 1.8 %broadcast_in_dim.85 = pred[128,660]{1,0:T(8,128)(4,1)S(1)} reshape(pred[16,8,30,22]{3,2,1,0:T(8,128)(4,1)S(1)} %broadcast_and_fusion.2) | data formatting | bytes 168960 | tf_op jit(solution)/shard_map/while/body/eval_jaxpr/jit(_where)/broadcast_in_dim | solution.py:124
  99.3 1.8 %fusion.216 = f32[4,128]{1,0:T(4,128)S(1)} fusion(pred[128,660]{0,1:T(8,128)(4,1)S(1)} %copy.119, bf16[3,660,4,64]{1,3,2,0:T(8,128)(2,1)} %get-tuple-element.184, s32[]{:T(128)} %get-tuple-element.172, bf16[3,128,4,64]{1,3,2,0:T(8,128)(2,1)S(1)} %get-tuple-element.183), kind=kOutput, calls=%fused_computation.258.clone.1 | convolution fusion | flops 44606100 | bytes 546816 | tf_op jit(solution)/shard_map/while/body/eval_jaxpr/sub | solution.py:125
  101.2 2.1 %fusion.217 = bf16[3,128,4,64]{1,3,2,0:T(8,128)(2,1)S(1)} fusion(bf16[3,128,4,64]{1,3,2,0:T(8,128)(2,1)S(1)} %get-tuple-element.173, s32[]{:T(128)} %get-tuple-element.172, f32[4,128]{1,0:T(4,128)S(1)} %fusion.216, bf16[3,660,4,64]{1,3,2,0:T(8,128)(2,1)} %get-tuple-element.182, pred[128,660]{0,1:T(8,128)(4,1)S(1)} %copy.119, ...), kind=kOutput, calls=%fused_computation.9.clone.1 | convolution fusion | flops 88231056 | bytes 1006592 | tf_op jit(solution)/shard_map/while/body/eval_jaxpr/hqk,khe->qhe/dot_general | solution.py:126
  103.6 1.8 %broadcast_in_dim.85 = pred[128,660]{1,0:T(8,128)(4,1)S(1)} reshape(pred[16,8,30,22]{3,2,1,0:T(8,128)(4,1)S(1)} %broadcast_and_fusion.2) | data formatting | bytes 168960 | tf_op jit(solution)/shard_map/while/body/eval_jaxpr/jit(_where)/broadcast_in_dim | solution.py:124
  105.6 1.8 %fusion.216 = f32[4,128]{1,0:T(4,128)S(1)} fusion(pred[128,660]{0,1:T(8,128)(4,1)S(1)} %copy.119, bf16[3,660,4,64]{1,3,2,0:T(8,128)(2,1)} %get-tuple-element.184, s32[]{:T(128)} %get-tuple-element.172, bf16[3,128,4,64]{1,3,2,0:T(8,128)(2,1)S(1)} %get-tuple-element.183), kind=kOutput, calls=%fused_computation.258.clone.1 | convolution fusion | flops 44606100 | bytes 546816 | tf_op jit(solution)/shard_map/while/body/eval_jaxpr/sub | solution.py:125
  107.5 2.1 %fusion.217 = bf16[3,128,4,64]{1,3,2,0:T(8,128)(2,1)S(1)} fusion(bf16[3,128,4,64]{1,3,2,0:T(8,128)(2,1)S(1)} %get-tuple-element.173, s32[]{:T(128)} %get-tuple-element.172, f32[4,128]{1,0:T(4,128)S(1)} %fusion.216, bf16[3,660,4,64]{1,3,2,0:T(8,128)(2,1)} %get-tuple-element.182, pred[128,660]{0,1:T(8,128)(4,1)S(1)} %copy.119, ...), kind=kOutput, calls=%fused_computation.9.clone.1 | convolution fusion | flops 88231056 | bytes 1006592 | tf_op jit(solution)/shard_map/while/body/eval_jaxpr/hqk,khe->qhe/dot_general | solution.py:126
  111.8 4.4 %fusion.72 = bf16[3,16,8,256]{3,2,1,0:T(8,128)(2,1)} fusion(f32[3,16,8,256]{3,2,1,0:T(8,128)S(1)} %get-tuple-element.119, f32[3,16,8,1024]{3,2,1,0:T(8,128)S(1)} %get-tuple-element.120, bf16[1024,256]{1,0:T(8,128)(2,1)S(1)} %copy-done.12, u16[3,8,1024]{2,1,0:T(8,128)(2,1)S(1)} %get-tuple-element.78, u16[3,8,1024]{2,1,0:T(8,128)(2,1)S(1)} %get-tuple-element.77), kind=kOutput, calls=%fused_computation.91 | convolution fusion | flops 229048320 | bytes 2785280 | tf_op jit(solution)/shard_map/dot_general | solution.py:36
  (93 shorter events, 23.9 us)
Async XLA Ops:
  0.0 9.1 %copy-start = (bf16[256,1024]{1,0:T(8,128)(2,1)S(1)}, bf16[256,1024]{1,0:T(8,128)(2,1)}, u32[]{:S(2)}) copy-start(bf16[256,1024]{1,0:T(8,128)(2,1)} %param.22) | copy-start | bytes 1572868
  7.6 0.9 copy-start.1
  7.6 1.0 copy-start.8
  9.2 1.0 copy-start.10
  10.2 4.6 %copy-start.2 = (bf16[256,768]{1,0:T(8,128)(2,1)S(1)}, bf16[256,768]{1,0:T(8,128)(2,1)}, u32[]{:S(2)}) copy-start(bf16[256,768]{1,0:T(8,128)(2,1)} %param.24) | copy-start | bytes 1179652
  14.8 5.4 %copy-start.9 = (s32[2]{0:T(128)S(1)}, s32[2]{0:T(128)}, u32[]{:S(2)}) copy-start(s32[2]{0:T(128)} %param.18) | copy-start | bytes 28
  16.0 13.8 %all-to-all-start = ((bf16[3,4,32,768]{3,2,0,1:T(8,128)(2,1)}), bf16[3,4,32,768]{3,2,0,1:T(8,128)(2,1)S(1)}, u32[]{:S(2)}, u32[]{:S(2)}) async-start(bf16[3,4,32,768]{3,2,0,1:T(8,128)(2,1)} %copy.52), calls=%async_computation | async-start | bytes 1179648 | tf_op jit(solution)/shard_map/all_to_all | solution.py:164
  32.4 9.8 %copy-start.6 = (bf16[256,256]{1,0:T(8,128)(2,1)S(1)}, bf16[256,256]{1,0:T(8,128)(2,1)}, u32[]{:S(2)}) copy-start(bf16[256,256]{1,0:T(8,128)(2,1)} %param.25) | copy-start | bytes 393220
  33.5 8.7 %all-to-all-start.1 = ((bf16[12,1,32,256]{3,2,1,0:T(8,128)(2,1)}), bf16[12,1,32,256]{3,2,1,0:T(8,128)(2,1)S(1)}, u32[]{:S(2)}, u32[]{:S(2)}) async-start(bf16[12,1,32,256]{3,2,1,0:T(8,128)(2,1)} %bitcast.22), calls=%async_computation.1 | async-start | bytes 393216 | tf_op jit(solution)/shard_map/all_to_all | solution.py:166
  42.8 11.7 %copy-start.3 = (bf16[256,768]{1,0:T(8,128)(2,1)S(1)}, bf16[256,768]{1,0:T(8,128)(2,1)}, u32[]{:S(2)}) copy-start(bf16[256,768]{1,0:T(8,128)(2,1)} %param.26) | copy-start | bytes 1179652
  43.0 5.3 %collective-permute-start = (bf16[3,7,8,256]{3,2,1,0:T(8,128)(2,1)S(1)}, bf16[3,7,8,256]{3,2,1,0:T(8,128)(2,1)S(1)}, u32[]{:S(2)}, u32[]{:S(2)}) collective-permute-start(bf16[3,7,8,256]{3,2,1,0:T(8,128)(2,1)S(1)} %get-tuple-element.105), channel_id=1, source_target_pairs={{0,4},{4,0},{1,5},{5,1},{2,6},{6,2},{3,7},{7,3},{8,12},{12,8},{9,1... | collective-permute-start | bytes 258056 | tf_op jit(solution)/shard_map/ppermute | solution.py:19
  45.2 4.5 %collective-permute-start.1 = (bf16[3,7,8,256]{3,2,1,0:T(8,128)(2,1)S(1)}, bf16[3,7,8,256]{3,2,1,0:T(8,128)(2,1)S(1)}, u32[]{:S(2)}, u32[]{:S(2)}) collective-permute-start(bf16[3,7,8,256]{3,2,1,0:T(8,128)(2,1)S(1)} %get-tuple-element.106), channel_id=1, source_target_pairs={{4,0},{0,4},{5,1},{1,5},{6,2},{2,6},{7,3},{3,7},{12,8},{8,12},{13,... | collective-permute-start | bytes 258056 | tf_op jit(solution)/shard_map/ppermute | solution.py:22
  50.6 13.6 %collective-permute-start.2 = (bf16[3,30,7,256]{3,2,1,0:T(8,128)(2,1)}, bf16[3,30,7,256]{3,2,1,0:T(8,128)(2,1)S(1)}, u32[]{:S(2)}, u32[]{:S(2)}) collective-permute-start(bf16[3,30,7,256]{3,2,1,0:T(8,128)(2,1)} %get-tuple-element.103), channel_id=1, source_target_pairs={{0,1},{1,2},{2,3},{3,0},{4,5},{5,6},{6,7},{7,4},{8,9},{9,10},{10,1... | collective-permute-start | bytes 967688 | tf_op jit(solution)/shard_map/ppermute | solution.py:19
  52.4 17.2 %collective-permute-start.3 = (bf16[3,30,7,256]{3,2,1,0:T(8,128)(2,1)S(1)}, bf16[3,30,7,256]{3,2,1,0:T(8,128)(2,1)S(1)}, u32[]{:S(2)}, u32[]{:S(2)}) collective-permute-start(bf16[3,30,7,256]{3,2,1,0:T(8,128)(2,1)S(1)} %get-tuple-element.104), channel_id=1, source_target_pairs={{1,0},{2,1},{3,2},{0,3},{5,4},{6,5},{7,6},{4,7},{9,8},{10,9},{11,1... | collective-permute-start | bytes 967688 | tf_op jit(solution)/shard_map/ppermute | solution.py:22
  86.9 3.8 %copy-start.4 = (bf16[3,128,4,64]{1,3,2,0:T(8,128)(2,1)S(1)}, bf16[3,128,4,64]{1,3,2,0:T(8,128)(2,1)}, u32[]{:S(2)}) copy-start(bf16[3,128,4,64]{1,3,2,0:T(8,128)(2,1)} %copy.64) | copy-start | bytes 589828
  86.9 3.8 %copy-start.5 = (bf16[3,128,4,64]{1,3,2,0:T(8,128)(2,1)S(1)}, bf16[3,128,4,64]{1,3,2,0:T(8,128)(2,1)}, u32[]{:S(2)}) copy-start(bf16[3,128,4,64]{1,3,2,0:T(8,128)(2,1)} %custom-call) | copy-start | bytes 589828
  90.7 19.5 %copy-start.7 = (bf16[256,256]{1,0:T(8,128)(2,1)S(1)}, bf16[256,256]{1,0:T(8,128)(2,1)}, u32[]{:S(2)}) copy-start(bf16[256,256]{1,0:T(8,128)(2,1)} %param.27) | copy-start | bytes 393220
  109.6 1.1 copy-start.11
  110.8 1.0 copy-start.12
where the time goes:
time: 117 us; the launch traced here: 116 us
  local copies, waits for them, and re-layouts  34.9 us (30%)
  waiting for transfers between devices  29.9 us (26%)
  matrix products  27.9 us (24%)
  starting transfers between devices  13.7 us (12%)
  other arithmetic  9.2 us (8%)
    dot_general x11, matrix products, project(): result = jnp.dot(flattened, matrix, preferred_element_type=jnp.float32)  13.6 us
    ppermute x2, waiting for transfers between devices, with_halo(): lax.ppermute(lax.slice_in_dim(block, block.shape[dim] - width, None, axis...  10.8 us
    unnamed x30, local copies, waits for them, and re-layouts  9.45 us
    all_to_all x1, waiting for transfers between devices, per_device(): lax.all_to_all(projected, 'member', split_axis=1, concat_axis=0, tiled=True)  7.65 us
    ppermute x2, waiting for transfers between devices, with_halo(): lax.ppermute(lax.slice_in_dim(block, 0, width, axis=dim), axis, backward)  6.82 us
    dot_general x3, matrix products, attend_member(): jnp.einsum('hqk,khe->qhe', weights, value_part, preferred_element_type=jn...  6.37 us
    broadcast_in_dim x6, local copies, waits for them, and re-layouts, attend_member(): scores = jnp.where(allowed[None], scores, -1e+30)  6.02 us
    sub x3, matrix products, attend_member(): weights = jax.nn.softmax(scores, axis=-1).astype(jnp.bfloat16)  5.55 us
  transfers between devices with their start and end apart: 6, of which 6 were waited for; matrix products, arithmetic and copies ran while one was open for 4% of the time, Pallas kernels for 0%

commit v1 on v0

v1 whole, which is shorter than its diff:
```python
import functools

import jax
import jax.numpy as jnp
from jax import lax
from jax.experimental import pallas as pl
from jax.experimental.pallas import tpu as pltpu
from jax.sharding import PartitionSpec as P

HEADS = 4
WIN = 8
LANES = 128
EPSILON = 1e-05
MASKED = -1e30
VMEM_LIMIT = 40 * 1024 * 1024

f32 = jnp.float32
bf16 = jnp.bfloat16


def normalize(stream):
    average = jnp.mean(stream, axis=-1, keepdims=True)
    centered = stream - average
    spread = jnp.mean(centered * centered, axis=-1, keepdims=True)
    return (centered * lax.rsqrt(spread + EPSILON)).astype(bf16)


def dot(a, b):
    return jnp.dot(a, b, preferred_element_type=f32)


def head_lanes(channels):
    return lax.broadcasted_iota(jnp.int32, (1, channels), 1) // (channels // HEADS)


def attend(query, key, value, bias):
    amount, channels = query.shape
    lanes = head_lanes(channels)
    scale = (channels // HEADS) ** (-0.5)
    stacked = jnp.concatenate(
        [query * jnp.where(lanes == head, scale, 0.0).astype(bf16) for head in range(HEADS)], axis=0
    )
    scores = lax.dot_general(stacked, key, (((1,), (1,)), ((), ())), preferred_element_type=f32)
    scores = scores.reshape(HEADS, amount, key.shape[0]) + bias[None]
    top = jnp.max(scores, axis=-1, keepdims=True)
    powers = jnp.exp(scores - top)
    total = jnp.sum(powers, axis=-1, keepdims=True)
    weights = (powers * (1.0 / total)).astype(bf16)
    mixed = dot(weights.reshape(HEADS * amount, key.shape[0]), value)
    result = mixed[:amount]
    for head in range(1, HEADS):
        result = jnp.where(lanes == head, mixed[head * amount : (head + 1) * amount], result)
    return result.astype(bf16)


def feed_forward(stream, up_ref, down_ref, chunk=256):
    normed = normalize(stream)
    total = stream
    for start in range(0, up_ref.shape[1], chunk):
        raw = dot(normed, up_ref[:, start : start + chunk])
        hidden = (0.5 * raw * (1.0 + lax.erf(raw * 0.5**0.5))).astype(bf16)
        total = total + dot(hidden, down_ref[start : start + chunk, :])
    return total


def window_kernel(
    shape, fields_ref, mask_ref, embed_ref, qkv_ref, out_ref, up_ref, down_ref,
    stream_ref, normed_ref, turned, held, attended,
):
    members, height, breadth, channels = shape
    rows = members * height
    for part in range(channels // LANES):
        turned[part] = fields_ref[:, part * LANES : (part + 1) * LANES].astype(f32)
    columns = []
    for column in range(breadth):
        taken = jnp.concatenate(
            [turned[part, pl.ds(column, rows, stride=breadth), :] for part in range(channels // LANES)],
            axis=1,
        ).reshape(members, height, channels)
        land = mask_ref[:, column : column + 1].astype(f32) * embed_ref[...]
        columns.append((taken + land[None]).reshape(rows, channels))
    stream = jnp.concatenate(columns, axis=0)
    held[...] = dot(normalize(stream), qkv_ref[...]).astype(bf16).reshape(breadth, rows, 3 * channels)
    tokens = breadth * height
    block = (lax.broadcasted_iota(jnp.int32, (tokens, tokens), 0) % height) // WIN
    other = (lax.broadcasted_iota(jnp.int32, (tokens, tokens), 1) % height) // WIN
    bias = jnp.where(block == other, 0.0, MASKED).astype(f32)
    for member in range(members):
        part = slice(member * height, (member + 1) * height)
        query, key, value = (
            held[:, part, i * channels : (i + 1) * channels].reshape(tokens, channels) for i in range(3)
        )
        attended[:, part, :] = attend(query, key, value, bias).reshape(breadth, height, channels)
    stream = stream + dot(attended[...].reshape(breadth * rows, channels), out_ref[...])
    stream = feed_forward(stream, up_ref, down_ref)
    stream_ref[...] = stream
    normed_ref[...] = normalize(stream)


def member_kernel(
    shape, stream_ref, *refs
):
    members, height, breadth, channels = shape
    *block_refs, qkv_ref, out_ref, late_ref, normed_ref, keys, queries, attended = refs
    rows = members * height
    amount = rows * len(block_refs)
    queries[...] = dot(block_refs[0][...], qkv_ref[:, :channels]).astype(bf16).reshape(
        breadth, rows, channels
    )
    for index, block_ref in enumerate(block_refs):
        keys[:, index * rows : (index + 1) * rows, :] = (
            dot(block_ref[...], qkv_ref[:, channels:]).astype(bf16).reshape(breadth, rows, 2 * channels)
        )
    row = lax.broadcasted_iota(jnp.int32, (rows, amount), 0) % height
    other = lax.broadcasted_iota(jnp.int32, (rows, amount), 1) % height
    bias = jnp.where(row == other, 0.0, MASKED).astype(f32)
    for column in range(breadth):
        attended[column] = attend(
            queries[column], keys[column, :, :channels], keys[column, :, channels:], bias
        )
    stream = stream_ref[...] + dot(attended[...].reshape(breadth * rows, channels), out_ref[...])
    late_ref[...] = stream
    normed_ref[...] = normalize(stream)


def shift_kernel(
    shape, place_ref, stream_ref, normed_ref, side_ref, edge_ref, corner_ref, qkv_ref, out_ref, up_ref,
    down_ref, updated_ref, held, beside, attended, turned,
):
    members, height, breadth, channels = shape
    rows, edge_rows = members * height, members * WIN
    tokens, edge_tokens = breadth * height, breadth * WIN
    held[...] = dot(normed_ref[...], qkv_ref[...]).astype(bf16).reshape(breadth, rows, 3 * channels)
    beside[...] = dot(side_ref[...], qkv_ref[:, channels:]).astype(bf16).reshape(
        breadth, rows, 2 * channels
    )
    edge = dot(edge_ref[...], qkv_ref[:, channels:]).reshape(breadth, edge_rows, 2 * channels)
    corner = dot(corner_ref[...], qkv_ref[:, channels:]).reshape(breadth, edge_rows, 2 * channels)

    lat_shift, lon_shift, first, last = place_ref[0], place_ref[1], place_ref[2], place_ref[3]
    amount = 2 * tokens + 2 * edge_tokens
    query_index = lax.broadcasted_iota(jnp.int32, (tokens, 1), 0)
    query_row, query_column = query_index % height, query_index // height
    query_tag = 2 * ((query_row - lat_shift + WIN) // WIN) + jnp.where(query_column >= lon_shift, 1, 0)
    index = lax.broadcasted_iota(jnp.int32, (1, amount), 1)
    whole = index < 2 * tokens
    local = jnp.where(whole, index % tokens, (index - 2 * tokens) % edge_tokens)
    mixed = jnp.where(whole, index // tokens, jnp.where(index < 2 * tokens + edge_tokens, 0, 1))
    key_row = jnp.where(whole, local % height, local % WIN)
    key_column = jnp.where(whole, local // height, local // WIN)
    edge_lat = jnp.where(
        key_row >= lat_shift, -1000 * first, height // WIN - 1000 * last
    )
    key_lat = jnp.where(whole, (key_row - lat_shift + WIN) // WIN, edge_lat)
    key_lon = jnp.where(key_column >= lon_shift, 1 - mixed, mixed)
    bias = jnp.where(query_tag == 2 * key_lat + key_lon, 0.0, MASKED).astype(f32)

    for member in range(members):
        part = slice(member * height, (member + 1) * height)
        edge_part = slice(member * WIN, (member + 1) * WIN)
        query = held[:, part, :channels].reshape(tokens, channels)
        pairs = []
        for i in range(2):
            lanes = slice(i * channels, (i + 1) * channels)
            lanes_held = slice((i + 1) * channels, (i + 2) * channels)
            pairs.append(
                jnp.concatenate(
                    [
                        held[:, part, lanes_held].reshape(tokens, channels),
                        beside[:, part, lanes].reshape(tokens, channels),
                        edge[:, edge_part, lanes].reshape(edge_tokens, channels).astype(bf16),
                        corner[:, edge_part, lanes].reshape(edge_tokens, channels).astype(bf16),
                    ],
                    axis=0,
                )
            )
        attended[:, part, :] = attend(query, pairs[0], pairs[1], bias).reshape(breadth, height, channels)
    stream = stream_ref[...] + dot(attended[...].reshape(breadth * rows, channels), out_ref[...])
    stream = feed_forward(stream, up_ref, down_ref)
    for column in range(breadth):
        for part in range(channels // LANES):
            turned[part, pl.ds(column, rows, stride=breadth), :] = stream[
                column * rows : (column + 1) * rows, part * LANES : (part + 1) * LANES
            ]
    for part in range(channels // LANES):
        updated_ref[:, part * LANES : (part + 1) * LANES] = turned[part].astype(bf16)


def in_vmem(count):
    return [pl.BlockSpec(memory_space=pltpu.VMEM)] * count


def per_device(
    fields, land_mask, offsets, land_embed, win_qkv, win_out, win_up, win_down, mem_qkv, mem_out,
    shift_qkv, shift_out, shift_up, shift_down,
):
    shape = fields.shape
    members, height, breadth, channels = shape
    rows, tokens = members * height, members * height * breadth
    params = pltpu.CompilerParams(vmem_limit_bytes=VMEM_LIMIT)
    stream, normed = pl.pallas_call(
        functools.partial(window_kernel, shape),
        out_shape=(
            jax.ShapeDtypeStruct((tokens, channels), f32),
            jax.ShapeDtypeStruct((tokens, channels), bf16),
        ),
        in_specs=in_vmem(7),
        out_specs=tuple(in_vmem(2)),
        scratch_shapes=[
            pltpu.VMEM((channels // LANES, tokens, LANES), f32),
            pltpu.VMEM((breadth, rows, 3 * channels), bf16),
            pltpu.VMEM((breadth, rows, channels), bf16),
        ],
        compiler_params=params,
    )(
        fields.reshape(tokens, channels), land_mask, land_embed.reshape(1, channels),
        win_qkv, win_out, win_up, win_down,
    )

    groups = lax.axis_size("member")
    blocks = [normed]
    bit = 1
    while bit < groups:
        bit *= 2
    while bit > 1:
        bit //= 2
        partner = [(i, i ^ bit) for i in range(groups)]
        blocks = blocks + [lax.ppermute(block, "member", partner) for block in blocks]

    late, normed = pl.pallas_call(
        functools.partial(member_kernel, shape),
        out_shape=(
            jax.ShapeDtypeStruct((tokens, channels), f32),
            jax.ShapeDtypeStruct((tokens, channels), bf16),
        ),
        in_specs=in_vmem(3 + len(blocks)),
        out_specs=tuple(in_vmem(2)),
        scratch_shapes=[
            pltpu.VMEM((breadth, rows * groups, 2 * channels), bf16),
            pltpu.VMEM((breadth, rows, channels), bf16),
            pltpu.VMEM((breadth, rows, channels), bf16),
        ],
        compiler_params=params,
    )(stream, *blocks, mem_qkv, mem_out)

    lat_count, lon_count = lax.axis_size("lat"), lax.axis_size("lon")
    lat_index = lax.axis_index("lat")
    ring = [(i, (i + 1) % lon_count) for i in range(lon_count)]
    back = [(b, a) for a, b in ring]
    own = normed.reshape(breadth, members, height, channels)
    top, bottom = own[:, :, :WIN], own[:, :, height - WIN :]
    down = [(i, i + 1) for i in range(lat_count - 1)]
    up = [(b, a) for a, b in down]
    if lat_count == 2:
        sends = [(jnp.where(lat_index == 0, bottom, top), down + up)]
    else:
        sends = [(bottom, down), (top, up)]

    def both_ways(amount, own, *edges):
        def along(block, lat_pairs):
            if lat_pairs is None:
                low = lax.ppermute(block[amount:], "lon", ring)
                high = lax.ppermute(block[:amount], "lon", back)
            else:
                low, high = (
                    lax.ppermute(
                        piece,
                        ("lat", "lon"),
                        [
                            (a * lon_count + c, b * lon_count + d)
                            for a, b in lat_pairs
                            for c, d in lon_pairs
                        ],
                    )
                    for piece, lon_pairs in ((block[amount:], ring), (block[:amount], back))
                )
            return jnp.concatenate([high, low], axis=0)

        straight = [lax.ppermute(block, "lat", pairs) for block, (_, pairs) in zip(edges, sends)]
        corners = [along(block, pairs) for block, (_, pairs) in zip(edges, sends)]
        return [along(own, None)] + straight + corners

    received = lax.switch(
        offsets[1] - 1,
        [functools.partial(both_ways, amount) for amount in range(1, WIN)],
        own, *[block for block, _ in sends],
    )
    side = received[0]
    count = len(sends)
    if count == 1:
        edge, corner = received[1], received[2]
    else:
        chosen = (jnp.arange(WIN, dtype=jnp.int32) >= offsets[0])[None, None, :, None]
        edge = jnp.where(chosen, received[1], received[2])
        corner = jnp.where(chosen, received[3], received[4])

    place = jnp.concatenate(
        [
            offsets,
            jnp.stack([lat_index == 0, lat_index == lat_count - 1]).astype(jnp.int32),
        ]
    )
    updated = pl.pallas_call(
        functools.partial(shift_kernel, shape),
        out_shape=jax.ShapeDtypeStruct((tokens, channels), bf16),
        in_specs=[pl.BlockSpec(memory_space=pltpu.SMEM)] + in_vmem(9),
        out_specs=pl.BlockSpec(memory_space=pltpu.VMEM),
        scratch_shapes=[
            pltpu.VMEM((breadth, rows, 3 * channels), bf16),
            pltpu.VMEM((breadth, rows, 2 * channels), bf16),
            pltpu.VMEM((breadth, rows, channels), bf16),
            pltpu.VMEM((channels // LANES, tokens, LANES), f32),
        ],
        compiler_params=params,
    )(
        place, late, normed, side.reshape(tokens, channels), edge.reshape(-1, channels),
        corner.reshape(-1, channels), shift_qkv, shift_out, shift_up, shift_down,
    )
    return updated.reshape(shape)


def solution(mesh):
    return jax.shard_map(
        per_device,
        mesh=mesh,
        in_specs=(P("member", "lat", "lon", None), P("lat", "lon")) + (P(),) * 12,
        out_specs=P("member", "lat", "lon", None),
        check_vma=False,
    )
```

time: 117 us -> 38.9 us (0.33); the launches traced: 116 us -> 39.5 us
  matrix products: 27.9 us -> 0 us
  local copies, waits for them, and re-layouts: 34.9 us -> 7.71 us
  waiting for transfers between devices: 29.9 us -> 10 us
  Pallas kernels: 0 us -> 9.29 us
  other arithmetic: 9.2 us -> 0.2 us
  starting transfers between devices: 13.7 us -> 11.4 us
    dot_general x17 -> x0, matrix products: 21 us -> none  [the longest x11 13.6 us: project(): result = jnp.dot(flattened, matrix, preferred_element_type=jnp.float32)]
    all_to_all x2 -> x0, waiting for transfers between devices: 12.3 us -> none  [the longest x1 7.65 us: per_device(): lax.all_to_all(projected, 'member', split_axis=1, concat_axis=0, tiled=True)]
    pallas_call x0 -> x3, Pallas kernels: none -> 9.29 us  [the longest x1 4.53 us: per_device(): pl.pallas_call(functools.partial(shift_kernel, shape), out_shape=jax.Shap...]
    reshape x6 -> x0, local copies, waits for them, and re-layouts: 9.05 us -> none  [the longest x1 3.32 us: shifted_attention(): value_heads = borders[..., channels:].reshape(members, -1, HEADS, head_size)]
    all_to_all x2 -> x0, starting transfers between devices: 7.6 us -> none  [the longest x1 4.24 us: per_device(): lax.all_to_all(projected, 'member', split_axis=1, concat_axis=0, tiled=True)]
    ppermute x4 -> x8, waiting for transfers between devices: 17.6 us -> 10 us  [the longest x3 4.17 us: per_device(): lax.ppermute(block, 'member', partner)]
    slice x8 -> x5, local copies, waits for them, and re-layouts: 8.19 us -> 0.68 us  [the longest x1 0.66 us: per_device(): offsets[1] - 1]
    sub x5 -> x0, matrix products: 6.91 us -> none  [the longest x3 5.55 us: attend_member(): weights = jax.nn.softmax(scores, axis=-1).astype(jnp.bfloat16)]
  transfers between devices with their start and end apart: 6 -> 8, of which waited for: 6 -> 4; matrix products, arithmetic and copies ran while one was open for 4% -> 2% of each run, Pallas kernels for 0% -> 0%
where the time goes in v1:
time: 38.9 us; the launch traced here: 39.5 us
  starting transfers between devices  11.4 us (29%)
  waiting for transfers between devices  10 us (26%)
  Pallas kernels  9.29 us (24%)
  local copies, waits for them, and re-layouts  7.71 us (20%)
  between operations  0.8 us (2%)
    unnamed x27, local copies, waits for them, and re-layouts  7.03 us
    ppermute x2, starting transfers between devices, along(): lax.ppermute(piece, ('lat', 'lon'), [(a * lon_count + c, b * lon_count +...  6.34 us
    pallas_call x1, Pallas kernels, per_device(): pl.pallas_call(functools.partial(shift_kernel, shape), out_shape=jax.Shap...  4.53 us
    ppermute x3, waiting for transfers between devices, per_device(): lax.ppermute(block, 'member', partner)  4.17 us
    ppermute x2, waiting for transfers between devices, along(): lax.ppermute(piece, ('lat', 'lon'), [(a * lon_count + c, b * lon_count +...  3.58 us
    ppermute x3, starting transfers between devices, per_device(): lax.ppermute(block, 'member', partner)  3.04 us
    pallas_call x1, Pallas kernels, per_device(): pl.pallas_call(functools.partial(window_kernel, shape), out_shape=(jax.Sh...  2.83 us
    ppermute x1, waiting for transfers between devices, along(): low = lax.ppermute(block[amount:], 'lon', ring)  2.29 us
  transfers between devices with their start and end apart: 8, of which 4 were waited for; matrix products, arithmetic and copies ran while one was open for 2% of the time, Pallas kernels for 0%

profile of v1, /device:TPU:0, one launch (start us, length us, event | category | flops | bytes accessed | tf_op | source)
XLA Modules:
  0.0 39.5 jit_solution(10172217546663234295)
XLA Ops:
  0.0 0.8 %copy.15.mask_ref = s32[16,8]{1,0:T(8,128)S(1)} copy(s32[16,8]{0,1:T(8,128)} %param.22) | data formatting | bytes 1024 | tf_op args[1]
  0.8 0.7 %copy-done.11 = f32[256]{0:T(256)S(1)} copy-done((f32[256]{0:T(256)S(1)}, f32[256]{0:T(256)}, u32[]{:S(2)}) %copy-start.11) | copy-done | bytes 1048
  1.4 1.0 %copy-done = bf16[256,1024]{1,0:T(8,128)(2,1)S(1)} copy-done((bf16[256,1024]{1,0:T(8,128)(2,1)S(1)}, bf16[256,1024]{1,0:T(8,128)(2,1)}, u32[]{:S(2)}) %copy-start) | copy-done | bytes 524312
  2.5 1.0 %copy-done.1 = bf16[1024,256]{1,0:T(8,128)(2,1)S(1)} copy-done((bf16[1024,256]{1,0:T(8,128)(2,1)S(1)}, bf16[1024,256]{1,0:T(8,128)(2,1)}, u32[]{:S(2)}) %copy-start.1) | copy-done | bytes 524312
  3.5 1.0 %copy-done.4 = bf16[256,768]{1,0:T(8,128)(2,1)S(1)} copy-done((bf16[256,768]{1,0:T(8,128)(2,1)S(1)}, bf16[256,768]{1,0:T(8,128)(2,1)}, u32[]{:S(2)}) %copy-start.4) | copy-done | bytes 393240
  4.5 0.9 %copy-done.7 = bf16[3,16,8,256]{3,2,1,0:T(8,128)(2,1)S(1)} copy-done((bf16[3,16,8,256]{3,2,1,0:T(8,128)(2,1)S(1)}, bf16[3,16,8,256]{3,2,1,0:T(8,128)(2,1)}, u32[]{:S(2)}) %copy-start.7) | copy-done | bytes 196632
  5.4 0.9 %copy-done.8 = bf16[256,256]{1,0:T(8,128)(2,1)S(1)} copy-done((bf16[256,256]{1,0:T(8,128)(2,1)S(1)}, bf16[256,256]{1,0:T(8,128)(2,1)}, u32[]{:S(2)}) %copy-start.8) | copy-done | bytes 131096
  6.4 2.8 %shard_map.136 = (f32[384,256]{1,0:T(8,128)S(1)}, bf16[384,256]{1,0:T(8,128)(2,1)S(1)}) custom-call(bf16[384,256]{1,0:T(8,128)(2,1)S(1)} %bitcast.28, s32[16,8]{1,0:T(8,128)S(1)} %copy.15.mask_ref, f32[1,256]{1,0:T(1,128)S(1)} %bitcast.29, bf16[256,768]{1,0:T(8,128)(2,1)S(1)} %copy-done.4, bf16[256,256]{1,0:T(8,128)(2,1)S(1)} %copy-done.8, ...), custom_call_target="tpu_custom_call" | custom-call | tf_op jit(solution)/shard_map/pallas_call | solution.py:201
  9.2 3.0 %collective-permute-start.35 = (bf16[384,256]{1,0:T(8,128)(2,1)S(1)}, bf16[384,256]{1,0:T(8,128)(2,1)S(1)}, u32[]{:S(2)}, u32[]{:S(2)}) collective-permute-start(bf16[384,256]{1,0:T(8,128)(2,1)S(1)} %get-tuple-element.100.refs_0_), channel_id=1, source_target_pairs={{0,16},{8,24},{16,0},{24,8},{1,17},{9,25},{17,1},{25,9},{2,18},{10... | collective-permute-start | bytes 589832 | tf_op jit(solution)/shard_map/ppermute | solution.py:228
  12.2 0.7 %copy-done.12 = s32[2]{0:T(128)S(1)} copy-done((s32[2]{0:T(128)S(1)}, s32[2]{0:T(128)}, u32[]{:S(2)}) %copy-start.12) | copy-done | bytes 32
  12.9 0.7 %slice.131 = s32[1]{0:T(128)} slice(s32[2]{0:T(128)S(1)} %copy-done.12), slice={[1:2]} | slice | bytes 8 | tf_op jit(solution)/shard_map/slice | solution.py:284
  14.2 2.9 %collective-permute-done.35.refs_1_ = bf16[384,256]{1,0:T(8,128)(2,1)S(1)} collective-permute-done((bf16[384,256]{1,0:T(8,128)(2,1)S(1)}, bf16[384,256]{1,0:T(8,128)(2,1)S(1)}, u32[]{:S(2)}, u32[]{:S(2)}) %collective-permute-start.35) | collective-permute-done | bytes 196640 | tf_op jit(solution)/shard_map/ppermute | solution.py:228
  17.1 0.1 add_convert_fusion
  17.2 0.1 pad_add_fusion.place_ref
  17.3 0.0 collective-permute-done.36.refs_2_
  17.3 1.3 %collective-permute-done.37.refs_3_ = bf16[384,256]{1,0:T(8,128)(2,1)S(1)} collective-permute-done((bf16[384,256]{1,0:T(8,128)(2,1)S(1)}, bf16[384,256]{1,0:T(8,128)(2,1)S(1)}, u32[]{:S(2)}, u32[]{:S(2)}) %collective-permute-start.37) | collective-permute-done | bytes 196640 | tf_op jit(solution)/shard_map/ppermute | solution.py:228
  18.6 1.9 %shard_map.137 = (f32[384,256]{1,0:T(8,128)S(1)}, bf16[384,256]{1,0:T(8,128)(2,1)S(1)}) custom-call(f32[384,256]{1,0:T(8,128)S(1)} %get-tuple-element.99.stream_ref, bf16[384,256]{1,0:T(8,128)(2,1)S(1)} %get-tuple-element.100.refs_0_, bf16[384,256]{1,0:T(8,128)(2,1)S(1)} %collective-permute-done.35.refs_1_, ...), custom_call_target="tpu_custom_call" | custom-call | tf_op jit(solution)/shard_map/pallas_call | solution.py:230
  20.5 0.0 copy-start.2
  20.5 0.0 copy-start.3
  20.5 0.0 copy-start.6
  20.5 0.0 copy-start.9
  20.6 14.4 %conditional.1 = (bf16[384,256]{1,0:T(8,128)(2,1)S(1)}, bf16[192,256]{1,0:T(8,128)(2,1)}, bf16[192,256]{1,0:T(8,128)(2,1)S(1)}) conditional(s32[]{:T(128)} %bitcast.25, (bf16[8,3,16,256]{3,2,1,0:T(8,128)(2,1)S(1)}, pred[]{:T(512)}) %tuple.64, (bf16[8,3,16,256]{3,2,1,0:T(8,128)(2,1)S(1)}, pred[]{:T(512)}) %tuple.65, ...), branch_computations={%region_0.1_spmd, %region_1.2_spmd, %region_2.3_spmd, %region_3.4_... | conditional | flops 196608 | bytes 3047649 | solution.py:283
  20.6 4.8 %collective-permute-start.23 = (bf16[6,3,8,256]{3,2,1,0:T(8,128)(2,1)S(1)}, bf16[6,3,8,256]{3,2,1,0:T(8,128)(2,1)S(1)}, u32[]{:S(2)}, u32[]{:S(2)}) collective-permute-start(bf16[6,3,8,256]{3,2,1,0:T(8,128)(2,1)S(1)} %slice.142), channel_id=1, source_target_pairs={{1,4},{2,5},{3,6},{0,7},{5,0},{6,1},{7,2},{4,3},{9,12},{10,13},{11... | collective-permute-start | bytes 221192 | tf_op jit(solution)/shard_map/cond/branch_5_fun/ppermute | solution.py:266
  25.4 0.5 %collective-permute-start.20 = (bf16[6,3,16,256]{3,2,1,0:T(8,128)(2,1)S(1)}, bf16[6,3,16,256]{3,2,1,0:T(8,128)(2,1)S(1)}, u32[]{:S(2)}, u32[]{:S(2)}) collective-permute-start(bf16[6,3,16,256]{3,2,1,0:T(8,128)(2,1)S(1)} %slice.118), channel_id=1, source_target_pairs={{1,0},{2,1},{3,2},{0,3},{5,4},{6,5},{7,6},{4,7},{9,8},{10,9},{11,1... | collective-permute-start | bytes 442376 | tf_op jit(solution)/shard_map/cond/branch_5_fun/ppermute | solution.py:263
  26.0 1.5 %collective-permute-start.24 = (bf16[2,3,8,256]{3,2,1,0:T(8,128)(2,1)S(1)}, bf16[2,3,8,256]{3,2,1,0:T(8,128)(2,1)S(1)}, u32[]{:S(2)}, u32[]{:S(2)}) collective-permute-start(bf16[2,3,8,256]{3,2,1,0:T(8,128)(2,1)S(1)} %slice.143), channel_id=1, source_target_pairs={{0,5},{1,6},{2,7},{3,4},{4,1},{5,2},{6,3},{7,0},{8,13},{9,14},{10,... | collective-permute-start | bytes 73736 | tf_op jit(solution)/shard_map/cond/branch_5_fun/ppermute | solution.py:266
  27.5 1.5 %collective-permute-start.22 = (bf16[8,3,8,256]{3,2,1,0:T(8,128)(2,1)S(1)}, bf16[8,3,8,256]{3,2,1,0:T(8,128)(2,1)}, u32[]{:S(2)}, u32[]{:S(2)}) collective-permute-start(bf16[8,3,8,256]{3,2,1,0:T(8,128)(2,1)S(1)} %slice_select_fusion.5), channel_id=1, source_target_pairs={{0,4},{4,0},{1,5},{5,1},{2,6},{6,2},{3,7},{7,3},{8,12},{12,8},{9,1... | collective-permute-start | bytes 294920 | tf_op jit(solution)/shard_map/cond/branch_5_fun/ppermute | solution.py:279
  29.0 0.0 collective-permute-start.21
  29.0 3.6 %collective-permute-done.24 = bf16[2,3,8,256]{3,2,1,0:T(8,128)(2,1)S(1)} collective-permute-done((bf16[2,3,8,256]{3,2,1,0:T(8,128)(2,1)S(1)}, bf16[2,3,8,256]{3,2,1,0:T(8,128)(2,1)S(1)}, u32[]{:S(2)}, u32[]{:S(2)}) %collective-permute-start.24) | collective-permute-done | bytes 24608 | tf_op jit(solution)/shard_map/cond/branch_5_fun/ppermute | solution.py:266
  32.6 0.0 collective-permute-done.23
  32.6 2.3 %collective-permute-done.21 = bf16[2,3,16,256]{3,2,1,0:T(8,128)(2,1)S(1)} collective-permute-done((bf16[2,3,16,256]{3,2,1,0:T(8,128)(2,1)S(1)}, bf16[2,3,16,256]{3,2,1,0:T(8,128)(2,1)S(1)}, u32[]{:S(2)}, u32[]{:S(2)}) %collective-permute-start.21) | collective-permute-done | bytes 49184 | tf_op jit(solution)/shard_map/cond/branch_5_fun/ppermute | solution.py:262
  34.9 0.0 collective-permute-done.20
  35.0 4.5 %shard_map.138 = bf16[384,256]{1,0:T(8,128)(2,1)} custom-call(s32[4]{0:T(128)S(1)} %pad_add_fusion.place_ref, f32[384,256]{1,0:T(8,128)S(1)} %get-tuple-element.101.stream_ref, bf16[384,256]{1,0:T(8,128)(2,1)S(1)} %get-tuple-element.102.normed_ref, bf16[384,256]{1,0:T(8,128)(2,1)S(1)} %get-tuple-element.103.side_ref, ...), custom_call_target="tpu_custom_call" | custom-call | tf_op jit(solution)/shard_map/pallas_call | solution.py:303
  (25 shorter events, 0.1 us)
Async XLA Ops:
  0.8 0.7 %copy-start.11 = (f32[256]{0:T(256)S(1)}, f32[256]{0:T(256)}, u32[]{:S(2)}) copy-start(f32[256]{0:T(256)} %param.24) | copy-start | bytes 3076
  1.4 1.0 %copy-start = (bf16[256,1024]{1,0:T(8,128)(2,1)S(1)}, bf16[256,1024]{1,0:T(8,128)(2,1)}, u32[]{:S(2)}) copy-start(bf16[256,1024]{1,0:T(8,128)(2,1)} %up_ref.2) | copy-start | bytes 1572868
  2.5 1.0 %copy-start.1 = (bf16[1024,256]{1,0:T(8,128)(2,1)S(1)}, bf16[1024,256]{1,0:T(8,128)(2,1)}, u32[]{:S(2)}) copy-start(bf16[1024,256]{1,0:T(8,128)(2,1)} %down_ref.2) | copy-start | bytes 1572868
  3.5 1.0 %copy-start.4 = (bf16[256,768]{1,0:T(8,128)(2,1)S(1)}, bf16[256,768]{1,0:T(8,128)(2,1)}, u32[]{:S(2)}) copy-start(bf16[256,768]{1,0:T(8,128)(2,1)} %qkv_ref.2) | copy-start | bytes 1179652
  4.5 0.9 %copy-start.7 = (bf16[3,16,8,256]{3,2,1,0:T(8,128)(2,1)S(1)}, bf16[3,16,8,256]{3,2,1,0:T(8,128)(2,1)}, u32[]{:S(2)}) copy-start(bf16[3,16,8,256]{3,2,1,0:T(8,128)(2,1)} %param.21) | copy-start | bytes 589828
  5.4 0.9 %copy-start.8 = (bf16[256,256]{1,0:T(8,128)(2,1)S(1)}, bf16[256,256]{1,0:T(8,128)(2,1)}, u32[]{:S(2)}) copy-start(bf16[256,256]{1,0:T(8,128)(2,1)} %out_ref.2) | copy-start | bytes 393220
  6.3 12.2 %copy-start.5 = (bf16[256,768]{1,0:T(8,128)(2,1)S(1)}, bf16[256,768]{1,0:T(8,128)(2,1)}, u32[]{:S(2)}) copy-start(bf16[256,768]{1,0:T(8,128)(2,1)} %refs_4_.1) | copy-start | bytes 1179652
  6.4 12.2 %copy-start.10 = (bf16[256,256]{1,0:T(8,128)(2,1)S(1)}, bf16[256,256]{1,0:T(8,128)(2,1)}, u32[]{:S(2)}) copy-start(bf16[256,256]{1,0:T(8,128)(2,1)} %refs_5_.1) | copy-start | bytes 393220
  9.2 7.9 %collective-permute-start.35 = (bf16[384,256]{1,0:T(8,128)(2,1)S(1)}, bf16[384,256]{1,0:T(8,128)(2,1)S(1)}, u32[]{:S(2)}, u32[]{:S(2)}) collective-permute-start(bf16[384,256]{1,0:T(8,128)(2,1)S(1)} %get-tuple-element.100.refs_0_), channel_id=1, source_target_pairs={{0,16},{8,24},{16,0},{24,8},{1,17},{9,25},{17,1},{25,9},{2,18},{10... | collective-permute-start | bytes 589832 | tf_op jit(solution)/shard_map/ppermute | solution.py:228
  12.2 5.1 %collective-permute-start.36 = (bf16[384,256]{1,0:T(8,128)(2,1)S(1)}, bf16[384,256]{1,0:T(8,128)(2,1)S(1)}, u32[]{:S(2)}, u32[]{:S(2)}) collective-permute-start(bf16[384,256]{1,0:T(8,128)(2,1)S(1)} %get-tuple-element.100.refs_0_), channel_id=1, source_target_pairs={{0,8},{8,0},{16,24},{24,16},{1,9},{9,1},{17,25},{25,17},{2,10},{10... | collective-permute-start | bytes 589832 | tf_op jit(solution)/shard_map/ppermute | solution.py:228
  12.2 0.7 %copy-start.12 = (s32[2]{0:T(128)S(1)}, s32[2]{0:T(128)}, u32[]{:S(2)}) copy-start(s32[2]{0:T(128)} %param.23) | copy-start | bytes 28
  17.1 1.4 %collective-permute-start.37 = (bf16[384,256]{1,0:T(8,128)(2,1)S(1)}, bf16[384,256]{1,0:T(8,128)(2,1)S(1)}, u32[]{:S(2)}, u32[]{:S(2)}) collective-permute-start(bf16[384,256]{1,0:T(8,128)(2,1)S(1)} %collective-permute-done.35.refs_1_), channel_id=1, source_target_pairs={{0,8},{8,0},{16,24},{24,16},{1,9},{9,1},{17,25},{25,17},{2,10},{10... | collective-permute-start | bytes 589832 | tf_op jit(solution)/shard_map/ppermute | solution.py:228
  20.5 14.4 %copy-start.2 = (bf16[256,1024]{1,0:T(8,128)(2,1)S(1)}, bf16[256,1024]{1,0:T(8,128)(2,1)}, u32[]{:S(2)}) copy-start(bf16[256,1024]{1,0:T(8,128)(2,1)} %up_ref.3) | copy-start | bytes 1572868
  20.5 14.4 %copy-start.3 = (bf16[1024,256]{1,0:T(8,128)(2,1)S(1)}, bf16[1024,256]{1,0:T(8,128)(2,1)}, u32[]{:S(2)}) copy-start(bf16[1024,256]{1,0:T(8,128)(2,1)} %down_ref.3) | copy-start | bytes 1572868
  20.5 14.4 %copy-start.6 = (bf16[256,768]{1,0:T(8,128)(2,1)S(1)}, bf16[256,768]{1,0:T(8,128)(2,1)}, u32[]{:S(2)}) copy-start(bf16[256,768]{1,0:T(8,128)(2,1)} %qkv_ref.3) | copy-start | bytes 1179652
  20.5 14.4 %copy-start.9 = (bf16[256,256]{1,0:T(8,128)(2,1)S(1)}, bf16[256,256]{1,0:T(8,128)(2,1)}, u32[]{:S(2)}) copy-start(bf16[256,256]{1,0:T(8,128)(2,1)} %out_ref.3) | copy-start | bytes 393220
  20.6 11.9 %collective-permute-start.23 = (bf16[6,3,8,256]{3,2,1,0:T(8,128)(2,1)S(1)}, bf16[6,3,8,256]{3,2,1,0:T(8,128)(2,1)S(1)}, u32[]{:S(2)}, u32[]{:S(2)}) collective-permute-start(bf16[6,3,8,256]{3,2,1,0:T(8,128)(2,1)S(1)} %slice.142), channel_id=1, source_target_pairs={{1,4},{2,5},{3,6},{0,7},{5,0},{6,1},{7,2},{4,3},{9,12},{10,13},{11... | collective-permute-start | bytes 221192 | tf_op jit(solution)/shard_map/cond/branch_5_fun/ppermute | solution.py:266
  25.4 9.4 %collective-permute-start.20 = (bf16[6,3,16,256]{3,2,1,0:T(8,128)(2,1)S(1)}, bf16[6,3,16,256]{3,2,1,0:T(8,128)(2,1)S(1)}, u32[]{:S(2)}, u32[]{:S(2)}) collective-permute-start(bf16[6,3,16,256]{3,2,1,0:T(8,128)(2,1)S(1)} %slice.118), channel_id=1, source_target_pairs={{1,0},{2,1},{3,2},{0,3},{5,4},{6,5},{7,6},{4,7},{9,8},{10,9},{11,1... | collective-permute-start | bytes 442376 | tf_op jit(solution)/shard_map/cond/branch_5_fun/ppermute | solution.py:263
  26.0 6.6 %collective-permute-start.24 = (bf16[2,3,8,256]{3,2,1,0:T(8,128)(2,1)S(1)}, bf16[2,3,8,256]{3,2,1,0:T(8,128)(2,1)S(1)}, u32[]{:S(2)}, u32[]{:S(2)}) collective-permute-start(bf16[2,3,8,256]{3,2,1,0:T(8,128)(2,1)S(1)} %slice.143), channel_id=1, source_target_pairs={{0,5},{1,6},{2,7},{3,4},{4,1},{5,2},{6,3},{7,0},{8,13},{9,14},{10,... | collective-permute-start | bytes 73736 | tf_op jit(solution)/shard_map/cond/branch_5_fun/ppermute | solution.py:266
  27.5 7.4 %collective-permute-start.22 = (bf16[8,3,8,256]{3,2,1,0:T(8,128)(2,1)S(1)}, bf16[8,3,8,256]{3,2,1,0:T(8,128)(2,1)}, u32[]{:S(2)}, u32[]{:S(2)}) collective-permute-start(bf16[8,3,8,256]{3,2,1,0:T(8,128)(2,1)S(1)} %slice_select_fusion.5), channel_id=1, source_target_pairs={{0,4},{4,0},{1,5},{5,1},{2,6},{6,2},{3,7},{7,3},{8,12},{12,8},{9,1... | collective-permute-start | bytes 294920 | tf_op jit(solution)/shard_map/cond/branch_5_fun/ppermute | solution.py:279
  29.0 5.9 %collective-permute-start.21 = (bf16[2,3,16,256]{3,2,1,0:T(8,128)(2,1)S(1)}, bf16[2,3,16,256]{3,2,1,0:T(8,128)(2,1)S(1)}, u32[]{:S(2)}, u32[]{:S(2)}) collective-permute-start(bf16[2,3,16,256]{3,2,1,0:T(8,128)(2,1)S(1)} %slice.119), channel_id=1, source_target_pairs={{0,1},{1,2},{2,3},{3,0},{4,5},{5,6},{6,7},{7,4},{8,9},{9,10},{10,1... | collective-permute-start | bytes 147464 | tf_op jit(solution)/shard_map/cond/branch_5_fun/ppermute | solution.py:262

commit v2 on v1

v2 whole, which is shorter than its diff:
```python
import functools

import jax
import jax.numpy as jnp
from jax import lax
from jax.experimental import pallas as pl
from jax.experimental.pallas import tpu as pltpu
from jax.sharding import PartitionSpec as P

HEADS = 4
WIN = 8
LANES = 128
EPSILON = 1e-05
MASKED = -1e30
VMEM_LIMIT = 40 * 1024 * 1024

f32 = jnp.float32
bf16 = jnp.bfloat16


def normalize(stream):
    average = jnp.mean(stream, axis=-1, keepdims=True)
    centered = stream - average
    spread = jnp.mean(centered * centered, axis=-1, keepdims=True)
    return (centered * lax.rsqrt(spread + EPSILON)).astype(bf16)


def dot(a, b):
    return jnp.dot(a, b, preferred_element_type=f32)


def head_lanes(channels):
    return lax.broadcasted_iota(jnp.int32, (1, channels), 1) // (channels // HEADS)


def attend(query, key, value, bias):
    amount, channels = query.shape
    lanes = head_lanes(channels)
    scale = (channels // HEADS) ** (-0.5)
    stacked = jnp.concatenate(
        [query * jnp.where(lanes == head, scale, 0.0).astype(bf16) for head in range(HEADS)], axis=0
    )
    scores = lax.dot_general(stacked, key, (((1,), (1,)), ((), ())), preferred_element_type=f32)
    scores = scores.reshape(HEADS, amount, key.shape[0]) + bias[None]
    top = jnp.max(scores, axis=-1, keepdims=True)
    powers = jnp.exp(scores - top)
    total = jnp.sum(powers, axis=-1, keepdims=True)
    weights = (powers * (1.0 / total)).astype(bf16)
    mixed = dot(weights.reshape(HEADS * amount, key.shape[0]), value)
    result = mixed[:amount]
    for head in range(1, HEADS):
        result = jnp.where(lanes == head, mixed[head * amount : (head + 1) * amount], result)
    return result.astype(bf16)


def feed_forward(stream, up_ref, down_ref, chunk=256):
    normed = normalize(stream)
    total = stream
    for start in range(0, up_ref.shape[1], chunk):
        raw = dot(normed, up_ref[:, start : start + chunk])
        hidden = (0.5 * raw * (1.0 + lax.erf(raw * 0.5**0.5))).astype(bf16)
        total = total + dot(hidden, down_ref[start : start + chunk, :])
    return total


def window_kernel(
    shape, *refs
):
    members, height, breadth, channels = shape
    sources, refs = refs[:7], refs[7:]
    stream_ref, normed_ref, *places, semaphores, turned, held, attended = refs
    copies = [
        pltpu.make_async_copy(source, place, semaphores.at[index])
        for index, (source, place) in enumerate(zip(sources, places))
    ]
    for copy in copies:
        copy.start()
    fields_ref, land_ref, embed_ref, qkv_ref, out_ref, up_ref, down_ref = places
    rows = members * height
    for copy in copies[:3]:
        copy.wait()
    for part in range(channels // LANES):
        turned[part] = fields_ref[:, part * LANES : (part + 1) * LANES].astype(f32)
    same = lax.broadcasted_iota(jnp.int32, (1, height, height), 1) == lax.broadcasted_iota(
        jnp.int32, (1, height, height), 2
    )
    land = jnp.sum(
        jnp.where(same, land_ref[...].astype(f32)[:, None, :], 0.0), axis=-1, keepdims=True
    )
    columns = []
    for column in range(breadth):
        taken = jnp.concatenate(
            [turned[part, pl.ds(column, rows, stride=breadth), :] for part in range(channels // LANES)],
            axis=1,
        ).reshape(members, height, channels)
        columns.append((taken + (land[column] * embed_ref[...])[None]).reshape(rows, channels))
    stream = jnp.concatenate(columns, axis=0)
    normed = normalize(stream)
    copies[3].wait()
    held[...] = dot(normed, qkv_ref[...]).astype(bf16).reshape(breadth, rows, 3 * channels)
    tokens = breadth * height
    block = (lax.broadcasted_iota(jnp.int32, (tokens, tokens), 0) % height) // WIN
    other = (lax.broadcasted_iota(jnp.int32, (tokens, tokens), 1) % height) // WIN
    bias = jnp.where(block == other, 0.0, MASKED).astype(f32)
    for member in range(members):
        part = slice(member * height, (member + 1) * height)
        query, key, value = (
            held[:, part, i * channels : (i + 1) * channels].reshape(tokens, channels) for i in range(3)
        )
        attended[:, part, :] = attend(query, key, value, bias).reshape(breadth, height, channels)
    for copy in copies[4:]:
        copy.wait()
    stream = stream + dot(attended[...].reshape(breadth * rows, channels), out_ref[...])
    stream = feed_forward(stream, up_ref, down_ref)
    stream_ref[...] = stream
    normed_ref[...] = normalize(stream)


def near_kernel(shape, *refs):
    members, height, breadth, channels = shape
    *block_refs, qkv_ref, queries_ref, pairs_ref = refs
    rows = members * height
    queries_ref[...] = (
        dot(block_refs[0][...], qkv_ref[:, :channels]).astype(bf16).reshape(breadth, rows, channels)
    )
    for index, block_ref in enumerate(block_refs):
        pairs_ref[:, index * rows : (index + 1) * rows, :] = (
            dot(block_ref[...], qkv_ref[:, channels:]).astype(bf16).reshape(breadth, rows, 2 * channels)
        )


def member_kernel(shape, lat_count, stream_ref, queries_ref, pairs_ref, *refs):
    members, height, breadth, channels = shape
    sides = 1 if lat_count == 2 else 2
    *block_refs, qkv_ref, out_ref = refs[: -4 - sides]
    late_ref, normed_ref, *edge_refs = refs[-4 - sides : -2]
    far, attended = refs[-2:]
    rows = members * height
    amount = rows * len(block_refs) + pairs_ref.shape[1]
    for index, block_ref in enumerate(block_refs):
        far[:, index * rows : (index + 1) * rows, :] = (
            dot(block_ref[...], qkv_ref[:, channels:]).astype(bf16).reshape(breadth, rows, 2 * channels)
        )
    row = lax.broadcasted_iota(jnp.int32, (rows, amount), 0) % height
    other = lax.broadcasted_iota(jnp.int32, (rows, amount), 1) % height
    bias = jnp.where(row == other, 0.0, MASKED).astype(f32)
    for column in range(breadth):
        both = jnp.concatenate([pairs_ref[column], far[column]], axis=0)
        attended[column] = attend(queries_ref[column], both[:, :channels], both[:, channels:], bias)
    stream = stream_ref[...] + dot(attended[...].reshape(breadth * rows, channels), out_ref[...])
    late_ref[...] = stream
    normed = normalize(stream)
    normed_ref[...] = normed
    lines = normed.astype(f32).reshape(breadth * members, height, channels)
    for edge_ref, edge in zip(edge_refs, lat_ends(lines, lat_count)):
        edge_ref[...] = edge.reshape(breadth * members * WIN, channels).astype(bf16)


def per_member(lines, members, breadth):
    lines = lines.reshape(breadth, members * WIN, lines.shape[-1])
    return [
        lines[:, member * WIN : (member + 1) * WIN].reshape(breadth * WIN, lines.shape[-1]).astype(bf16)
        for member in range(members)
    ]


def join_kernel(shape, lat_count, amount, first_ref, second_ref, side_ref, *end_refs):
    members, height, breadth, channels = shape
    high_ref, low_ref = (first_ref, second_ref) if 2 * amount <= breadth else (second_ref, first_ref)
    side_ref[:amount] = high_ref[...]
    side_ref[amount:] = low_ref[...]
    for part, block_ref in ((slice(0, amount), high_ref), (slice(amount, breadth), low_ref)):
        columns = part.stop - part.start
        lines = block_ref[...].astype(f32).reshape(columns * members, height, channels)
        for end_ref, end in zip(end_refs, lat_ends(lines, lat_count)):
            place = slice(part.start * members * WIN, part.stop * members * WIN)
            end_ref[place, :] = end.reshape(columns * members * WIN, channels).astype(bf16)


def lat_ends(lines, lat_count):
    top, bottom = lines[:, :WIN], lines[:, lines.shape[1] - WIN :]
    if lat_count == 2:
        return [jnp.where(lax.axis_index("lat") == 0, bottom, top)]
    return [bottom, top]


def early_kernel(shape, normed_ref, side_ref, edge_ref, qkv_ref, held_ref, beside_ref, across_ref):
    members, height, breadth, channels = shape
    rows = members * height
    held_ref[...] = dot(normed_ref[...], qkv_ref[...]).astype(bf16).reshape(breadth, rows, 3 * channels)
    beside_ref[...] = dot(side_ref[...], qkv_ref[:, channels:]).astype(bf16).reshape(
        breadth, rows, 2 * channels
    )
    edge = per_member(dot(edge_ref[...], qkv_ref[:, channels:]), members, breadth)
    for member in range(members):
        across_ref[member] = edge[member]


def corner_kernel(shape, corner_ref, qkv_ref, corner_pairs_ref):
    members, height, breadth, channels = shape
    corner = per_member(dot(corner_ref[...], qkv_ref[:, channels:]), members, breadth)
    for member in range(members):
        corner_pairs_ref[member] = corner[member]


def shift_kernel(
    shape, lat_count, place_ref, stream_ref, held, beside, across, corner, out_ref, up_ref, down_ref,
    updated_ref, attended, turned,
):
    members, height, breadth, channels = shape
    rows = members * height
    tokens, edge_tokens = breadth * height, breadth * WIN

    lat_shift, lon_shift = place_ref[0], place_ref[1]
    first = jnp.where(lax.axis_index("lat") == 0, 1, 0)
    last = jnp.where(lax.axis_index("lat") == lat_count - 1, 1, 0)
    amount = 2 * tokens + 2 * edge_tokens
    query_index = lax.broadcasted_iota(jnp.int32, (tokens, 1), 0)
    query_row, query_column = query_index % height, query_index // height
    query_tag = 2 * ((query_row - lat_shift + WIN) // WIN) + jnp.where(query_column >= lon_shift, 1, 0)
    index = lax.broadcasted_iota(jnp.int32, (1, amount), 1)
    whole = index < 2 * tokens
    local = jnp.where(whole, index % tokens, (index - 2 * tokens) % edge_tokens)
    mixed = jnp.where(whole, index // tokens, jnp.where(index < 2 * tokens + edge_tokens, 0, 1))
    key_row = jnp.where(whole, local % height, local % WIN)
    key_column = jnp.where(whole, local // height, local // WIN)
    edge_lat = jnp.where(key_row >= lat_shift, -1000 * first, height // WIN - 1000 * last)
    key_lat = jnp.where(whole, (key_row - lat_shift + WIN) // WIN, edge_lat)
    key_lon = jnp.where(key_column >= lon_shift, 1 - mixed, mixed)
    bias = jnp.where(query_tag == 2 * key_lat + key_lon, 0.0, MASKED).astype(f32)

    for member in range(members):
        part = slice(member * height, (member + 1) * height)
        query = held[:, part, :channels].reshape(tokens, channels)
        pairs = []
        for i in range(2):
            lanes = slice(i * channels, (i + 1) * channels)
            pairs.append(
                jnp.concatenate(
                    [
                        held[:, part, (i + 1) * channels : (i + 2) * channels].reshape(tokens, channels),
                        beside[:, part, lanes].reshape(tokens, channels),
                        across[member, :, lanes],
                        corner[member, :, lanes],
                    ],
                    axis=0,
                )
            )
        attended[:, part, :] = attend(query, pairs[0], pairs[1], bias).reshape(breadth, height, channels)
    stream = stream_ref[...] + dot(attended[...].reshape(breadth * rows, channels), out_ref[...])
    stream = feed_forward(stream, up_ref, down_ref)
    for column in range(breadth):
        for part in range(channels // LANES):
            turned[part, pl.ds(column, rows, stride=breadth), :] = stream[
                column * rows : (column + 1) * rows, part * LANES : (part + 1) * LANES
            ]
    for part in range(channels // LANES):
        updated_ref[:, part * LANES : (part + 1) * LANES] = turned[part].astype(bf16)


def in_vmem(count):
    return [pl.BlockSpec(memory_space=pltpu.VMEM)] * count


def per_device(
    fields, land_mask, offsets, land_embed, win_qkv, win_out, win_up, win_down, mem_qkv, mem_out,
    shift_qkv, shift_out, shift_up, shift_down,
):
    shape = fields.shape
    members, height, breadth, channels = shape
    rows, tokens = members * height, members * height * breadth
    edge_tokens = members * WIN * breadth
    params = pltpu.CompilerParams(vmem_limit_bytes=VMEM_LIMIT)
    sources = (
        fields.reshape(tokens, channels), land_mask.T, land_embed.reshape(1, channels),
        win_qkv, win_out, win_up, win_down,
    )
    stream, normed = pl.pallas_call(
        functools.partial(window_kernel, shape),
        out_shape=(
            jax.ShapeDtypeStruct((tokens, channels), f32),
            jax.ShapeDtypeStruct((tokens, channels), bf16),
        ),
        in_specs=[pl.BlockSpec(memory_space=pltpu.HBM)] * len(sources),
        out_specs=tuple(in_vmem(2)),
        scratch_shapes=[pltpu.VMEM(source.shape, source.dtype) for source in sources]
        + [
            pltpu.SemaphoreType.DMA((len(sources),)),
            pltpu.VMEM((channels // LANES, tokens, LANES), f32),
            pltpu.VMEM((breadth, rows, 3 * channels), bf16),
            pltpu.VMEM((breadth, rows, channels), bf16),
        ],
        compiler_params=pltpu.CompilerParams(vmem_limit_bytes=60 * 1024 * 1024),
    )(*sources)

    groups = lax.axis_size("member")
    blocks = [normed]
    bit = 1
    while bit * 2 < groups:
        bit *= 2
    far = [lax.ppermute(normed, "member", [(i, i ^ bit) for i in range(groups)])]
    near = []
    partners = []
    while bit > 1:
        bit //= 2
        partners.append([(i, i ^ bit) for i in range(groups)])
        near = near + [lax.ppermute(block, "member", partners[-1]) for block in blocks + near]

    queries, pairs = pl.pallas_call(
        functools.partial(near_kernel, shape),
        out_shape=(
            jax.ShapeDtypeStruct((breadth, rows, channels), bf16),
            jax.ShapeDtypeStruct((breadth, rows * len(blocks), 2 * channels), bf16),
        ),
        in_specs=in_vmem(1 + len(blocks)),
        out_specs=tuple(in_vmem(2)),
        compiler_params=params,
        cost_estimate=pl.CostEstimate(
            flops=2 * tokens * channels * channels * (1 + 2 * len(blocks)),
            bytes_accessed=2 * tokens * channels * 6,
            transcendentals=0,
        ),
    )(*blocks, mem_qkv)
    branch = offsets[1] - 1
    far[0], branch, queries, pairs = lax.optimization_barrier((far[0], branch, queries, pairs))
    for partner in partners:
        far = far + [lax.ppermute(block, "member", partner) for block in far]
    far = near + far

    lat_count, lon_count = lax.axis_size("lat"), lax.axis_size("lon")
    lat_index = lax.axis_index("lat")
    down = [(i, i + 1) for i in range(lat_count - 1)]
    up = [(b, a) for a, b in down]
    lat_pairs = [down + up] if lat_count == 2 else [down, up]
    late, normed, *edges = pl.pallas_call(
        functools.partial(member_kernel, shape, lat_count),
        out_shape=(
            jax.ShapeDtypeStruct((tokens, channels), f32),
            jax.ShapeDtypeStruct((tokens, channels), bf16),
        )
        + (jax.ShapeDtypeStruct((edge_tokens, channels), bf16),) * len(lat_pairs),
        in_specs=in_vmem(5 + len(far)),
        out_specs=tuple(in_vmem(2 + len(lat_pairs))),
        scratch_shapes=[
            pltpu.VMEM((breadth, rows * len(far), 2 * channels), bf16),
            pltpu.VMEM((breadth, rows, channels), bf16),
        ],
        compiler_params=params,
    )(stream, queries, pairs, *far, mem_qkv, mem_out)

    ring = [(i, (i + 1) % lon_count) for i in range(lon_count)]
    back = [(b, a) for a, b in ring]

    def gather(amount, own, *edges):
        low = lax.ppermute(own[amount:], "lon", ring)
        high = lax.ppermute(own[:amount], "lon", back)
        straight = [lax.ppermute(edge, "lat", pairs) for edge, pairs in zip(edges, lat_pairs)]
        end_shape = jax.ShapeDtypeStruct((edge_tokens, channels), bf16)
        side, *ends = pl.pallas_call(
            functools.partial(join_kernel, shape, lat_count, amount),
            out_shape=(jax.ShapeDtypeStruct((breadth, rows, channels), bf16),)
            + (end_shape,) * len(lat_pairs),
            in_specs=in_vmem(2),
            out_specs=tuple(in_vmem(1 + len(lat_pairs))),
            compiler_params=params,
        )(*((high, low) if 2 * amount <= breadth else (low, high)))
        corners = [lax.ppermute(end, "lat", pairs) for end, pairs in zip(ends, lat_pairs)]
        if lat_count == 2:
            edge, corner = straight[0], corners[0]
        else:
            above = jnp.tile(jnp.arange(WIN, dtype=jnp.int32) >= offsets[0], breadth * members)[:, None]
            edge, corner = jnp.where(above, *straight), jnp.where(above, *corners)

        pairs_shape = jax.ShapeDtypeStruct((members, breadth * WIN, 2 * channels), bf16)
        corner = pl.pallas_call(
            functools.partial(corner_kernel, shape),
            out_shape=pairs_shape,
            in_specs=in_vmem(2),
            out_specs=in_vmem(1)[0],
            compiler_params=params,
        )(corner, shift_qkv)
        return pl.pallas_call(
            functools.partial(early_kernel, shape),
            out_shape=(
                jax.ShapeDtypeStruct((breadth, rows, 3 * channels), bf16),
                jax.ShapeDtypeStruct((breadth, rows, 2 * channels), bf16),
                pairs_shape,
            ),
            in_specs=in_vmem(4),
            out_specs=tuple(in_vmem(3)),
            compiler_params=params,
            cost_estimate=pl.CostEstimate(
                flops=2 * tokens * channels * channels * 6,
                bytes_accessed=2 * tokens * channels * 8,
                transcendentals=0,
            ),
        )(own.reshape(tokens, channels), side.reshape(tokens, channels), edge, shift_qkv) + (corner,)

    held, beside, across, corner = lax.switch(
        branch,
        [functools.partial(gather, amount) for amount in range(1, WIN)],
        normed.reshape(breadth, rows, channels), *edges,
    )
    updated = pl.pallas_call(
        functools.partial(shift_kernel, shape, lat_count),
        out_shape=jax.ShapeDtypeStruct((tokens, channels), bf16),
        in_specs=[pl.BlockSpec(memory_space=pltpu.SMEM)] + in_vmem(8),
        out_specs=pl.BlockSpec(memory_space=pltpu.VMEM),
        scratch_shapes=[
            pltpu.VMEM((breadth, rows, channels), bf16),
            pltpu.VMEM((channels // LANES, tokens, LANES), f32),
        ],
        compiler_params=params,
    )(
        offsets, late, held, beside, across, corner, shift_out, shift_up, shift_down,
    )
    return updated.reshape(shape)


def solution(mesh):
    return jax.shard_map(
        per_device,
        mesh=mesh,
        in_specs=(P("member", "lat", "lon", None), P("lat", "lon")) + (P(),) * 12,
        out_specs=P("member", "lat", "lon", None),
        check_vma=False,
    )
```

time: 38.9 us -> 34.3 us (0.88)
  local copies, waits for them, and re-layouts: 7.71 us -> 1.62 us
  Pallas kernels: 9.29 us -> 11.3 us
  starting transfers between devices: 11.4 us -> 10 us
  waiting for transfers between devices: 10 us -> 11 us
    unnamed x27 -> x18, local copies, waits for them, and re-layouts: 7.03 us -> 0.96 us
    pallas_call x1, Pallas kernels: 2.83 us -> 4.64 us  [per_device(): pl.pallas_call(functools.partial(window_kernel, shape), out_shape=(jax.Sh...]
    ppermute x8 -> x7, starting transfers between devices: 11.4 us -> 10 us  [the longest x1 3.87 us: gather(): high = lax.ppermute(own[:amount], 'lon', back)]
    ppermute x8 -> x7, waiting for transfers between devices: 10 us -> 11 us  [the longest x1 4.33 us: gather(): low = lax.ppermute(own[amount:], 'lon', ring)]
    pallas_call x2 -> x6, Pallas kernels: 6.47 us -> 6.66 us  [the longest x1 3.91 us: per_device(): pl.pallas_call(functools.partial(shift_kernel, shape, lat_count), out_sha...]
  transfers between devices with their start and end apart: 8 -> 7, of which waited for: 4 -> 4; matrix products, arithmetic and copies ran while one was open for 2% -> 2% of each run, Pallas kernels for 0% -> 2%
where the time goes in v2:
time: 34.3 us; the launch traced here: 34.7 us
  Pallas kernels  11.3 us (33%)
  waiting for transfers between devices  11 us (32%)
  starting transfers between devices  10 us (29%)
  local copies, waits for them, and re-layouts  1.62 us (5%)
  between operations  0.74 us (2%)
    pallas_call x1, Pallas kernels, per_device(): pl.pallas_call(functools.partial(window_kernel, shape), out_shape=(jax.Sh...  4.64 us
    ppermute x1, waiting for transfers between devices, gather(): low = lax.ppermute(own[amount:], 'lon', ring)  4.33 us
    pallas_call x1, Pallas kernels, per_device(): pl.pallas_call(functools.partial(shift_kernel, shape, lat_count), out_sha...  3.91 us
    ppermute x1, starting transfers between devices, gather(): high = lax.ppermute(own[:amount], 'lon', back)  3.87 us
    ppermute x1, starting transfers between devices, per_device(): lax.ppermute(normed, 'member', [(i, i ^ bit) for i in range(groups)])  3.03 us
    ppermute x1, waiting for transfers between devices, gather(): lax.ppermute(end, 'lat', pairs)  2.64 us
    ppermute x1, waiting for transfers between devices, per_device(): lax.ppermute(normed, 'member', [(i, i ^ bit) for i in range(groups)])  2.58 us
    pallas_call x1, Pallas kernels, per_device(): pl.pallas_call(functools.partial(member_kernel, shape, lat_count), out_sh...  1.71 us
  transfers between devices with their start and end apart: 7, of which 4 were waited for; matrix products, arithmetic and copies ran while one was open for 2% of the time, Pallas kernels for 2%

profile of v2, /device:TPU:0, one launch (start us, length us, event | category | flops | bytes accessed | tf_op | source)
XLA Modules:
  0.0 34.7 jit_solution(5945313294393454918)
XLA Ops:
  0.0 4.6 %shard_map.136 = (f32[384,256]{1,0:T(8,128)}, bf16[384,256]{1,0:T(8,128)(2,1)}) custom-call(bf16[384,256]{1,0:T(8,128)(2,1)} %bitcast.40, s32[8,16]{1,0:T(8,128)} %bitcast.41, f32[1,256]{1,0:T(1,128)} %bitcast.42, bf16[256,768]{1,0:T(8,128)(2,1)} %refs_3_.2, bf16[256,256]{1,0:T(8,128)(2,1)} %refs_4_.2, bf16[256,1024]{1,0:T(8,128)(2,1)} %refs_5_.1, ...), custom_call_target="tpu_custom_call" | custom-call | tf_op jit(solution)/shard_map/pallas_call | solution.py:278
  4.7 0.0 copy-start.3
  4.7 3.0 %collective-permute-start.28 = (bf16[384,256]{1,0:T(8,128)(2,1)}, bf16[384,256]{1,0:T(8,128)(2,1)S(1)}, u32[]{:S(2)}, u32[]{:S(2)}) collective-permute-start(bf16[384,256]{1,0:T(8,128)(2,1)} %get-tuple-element.140.refs_0_), channel_id=1, source_target_pairs={{0,16},{8,24},{16,0},{24,8},{1,17},{9,25},{17,1},{25,9},{2,18},{10... | collective-permute-start | bytes 589832 | tf_op jit(solution)/shard_map/ppermute | solution.py:301
  7.7 0.0 collective-permute-start.29
  7.7 0.0 copy-done.7
  7.7 0.6 %slice.45 = s32[1]{0:T(128)} slice(s32[2]{0:T(128)S(1)} %copy-done.7), slice={[1:2]} | slice | bytes 8 | tf_op jit(solution)/shard_map/slice | solution.py:324
  9.0 0.0 copy-done
  9.0 0.0 copy-start.4
  9.0 0.9 %copy-done.4 = bf16[384,256]{1,0:T(8,128)(2,1)S(1)} copy-done((bf16[384,256]{1,0:T(8,128)(2,1)S(1)}, bf16[384,256]{1,0:T(8,128)(2,1)}, u32[]{:S(2)}) %copy-start.4) | copy-done | bytes 196632
  9.9 0.3 shard_map.137
  10.2 2.6 %collective-permute-done.28.refs_1_ = bf16[384,256]{1,0:T(8,128)(2,1)S(1)} collective-permute-done((bf16[384,256]{1,0:T(8,128)(2,1)}, bf16[384,256]{1,0:T(8,128)(2,1)S(1)}, u32[]{:S(2)}, u32[]{:S(2)}) %collective-permute-start.28) | collective-permute-done | bytes 196640 | tf_op jit(solution)/shard_map/ppermute | solution.py:301
  12.8 0.0 collective-permute-start.30
  12.8 0.0 collective-permute-done.29.refs_0_
  12.8 1.4 %collective-permute-done.30.refs_2_ = bf16[384,256]{1,0:T(8,128)(2,1)S(1)} collective-permute-done((bf16[384,256]{1,0:T(8,128)(2,1)S(1)}, bf16[384,256]{1,0:T(8,128)(2,1)S(1)}, u32[]{:S(2)}, u32[]{:S(2)}) %collective-permute-start.30) | collective-permute-done | bytes 196640 | tf_op jit(solution)/shard_map/ppermute | solution.py:327
  14.3 0.0 copy-done.3
  14.3 0.0 copy-done.5
  14.3 1.7 %shard_map.138 = (f32[384,256]{1,0:T(8,128)S(1)}, bf16[384,256]{1,0:T(8,128)(2,1)S(1)}, bf16[192,256]{1,0:T(8,128)(2,1)S(1)}) custom-call(f32[384,256]{1,0:T(8,128)S(1)} %copy-done.3, bf16[8,48,256]{2,1,0:T(8,128)(2,1)S(1)} %get-tuple-element.143.queries_ref, bf16[8,48,512]{2,1,0:T(8,128)(2,1)S(1)} %get-tuple-element.144.pairs_ref, ...), custom_call_target="tpu_custom_call" | custom-call | tf_op jit(solution)/shard_map/pallas_call | solution.py:335
  16.0 0.0 copy-start.1
  16.0 0.0 copy-start.2
  16.0 0.0 copy-start.6
  16.0 14.8 %conditional.1 = (bf16[8,48,768]{2,1,0:T(8,128)(2,1)S(1)}, bf16[8,48,512]{2,1,0:T(8,128)(2,1)S(1)}, bf16[3,64,512]{2,1,0:T(8,128)(2,1)S(1)}, bf16[3,64,512]{2,1,0:T(8,128)(2,1)S(1)}) conditional(s32[]{:T(128)} %clamp.3, (bf16[8,48,256]{2,1,0:T(8,128)(2,1)S(1)}, bf16[192,256]{1,0:T(8,128)(2,1)S(1)}, ...), branch_computations={%region_0.0_spmd, %region_1.0_spmd, %region_2.0_spmd, %region_3.0_... | conditional | flops 301989888 | bytes 3539136 | solution.py:399
  16.1 3.9 %collective-permute-start.17 = (bf16[6,48,256]{2,1,0:T(8,128)(2,1)S(1)}, bf16[6,48,256]{2,1,0:T(8,128)(2,1)S(1)}, u32[]{:S(2)}, u32[]{:S(2)}) collective-permute-start(bf16[6,48,256]{2,1,0:T(8,128)(2,1)S(1)} %slice.41), channel_id=1, source_target_pairs={{1,0},{2,1},{3,2},{0,3},{5,4},{6,5},{7,6},{4,7},{9,8},{10,9},{11,1... | collective-permute-start | bytes 442376 | tf_op jit(solution)/shard_map/cond/branch_5_fun/ppermute | solution.py:356
  20.0 0.0 collective-permute-start.16
  20.0 1.5 %collective-permute-start.18 = (bf16[192,256]{1,0:T(8,128)(2,1)S(1)}, bf16[192,256]{1,0:T(8,128)(2,1)S(1)}, u32[]{:S(2)}, u32[]{:S(2)}) collective-permute-start(bf16[192,256]{1,0:T(8,128)(2,1)S(1)} %get-tuple-element.109), channel_id=1, source_target_pairs={{0,4},{4,0},{1,5},{5,1},{2,6},{6,2},{3,7},{7,3},{8,12},{12,8},{9,1... | collective-permute-start | bytes 294920 | tf_op jit(solution)/shard_map/cond/branch_5_fun/ppermute | solution.py:357
  21.5 4.3 %collective-permute-done.16.first_ref = bf16[2,48,256]{2,1,0:T(8,128)(2,1)S(1)} collective-permute-done((bf16[2,48,256]{2,1,0:T(8,128)(2,1)S(1)}, bf16[2,48,256]{2,1,0:T(8,128)(2,1)S(1)}, u32[]{:S(2)}, u32[]{:S(2)}) %collective-permute-start.16) | collective-permute-done | bytes 49184 | tf_op jit(solution)/shard_map/cond/branch_5_fun/ppermute | solution.py:355
  25.8 0.0 collective-permute-done.17.second_ref
  25.9 1.6 %collective-permute-start.19 = (bf16[192,256]{1,0:T(8,128)(2,1)S(1)}, bf16[192,256]{1,0:T(8,128)(2,1)S(1)}, u32[]{:S(2)}, u32[]{:S(2)}) collective-permute-start(bf16[192,256]{1,0:T(8,128)(2,1)S(1)} %get-tuple-element.114), channel_id=1, source_target_pairs={{0,4},{4,0},{1,5},{5,1},{2,6},{6,2},{3,7},{7,3},{8,12},{12,8},{9,1... | collective-permute-start | bytes 294920 | tf_op jit(solution)/shard_map/cond/branch_5_fun/ppermute | solution.py:367
  27.4 0.0 collective-permute-done.18.edge_ref
  27.4 0.5 %branch_5_fun.4 = (bf16[8,48,768]{2,1,0:T(8,128)(2,1)S(1)}, bf16[8,48,512]{2,1,0:T(8,128)(2,1)S(1)}, bf16[3,64,512]{2,1,0:T(8,128)(2,1)S(1)}) custom-call(bf16[384,256]{1,0:T(8,128)(2,1)S(1)} %get-tuple-element.106.normed_ref, bf16[384,256]{1,0:T(8,128)(2,1)S(1)} %bitcast.18, bf16[192,256]{1,0:T(8,128)(2,1)S(1)} %collective-permute-done.18.edge_ref, ...), custom_call_target="tpu_custom_call" | custom-call | flops 301989888 | bytes 1572864 | tf_op jit(solution)/shard_map/cond/branch_5_fun/pallas_call | solution.py:382
  27.9 2.6 %collective-permute-done.19.corner_ref = bf16[192,256]{1,0:T(8,128)(2,1)S(1)} collective-permute-done((bf16[192,256]{1,0:T(8,128)(2,1)S(1)}, bf16[192,256]{1,0:T(8,128)(2,1)S(1)}, u32[]{:S(2)}, u32[]{:S(2)}) %collective-permute-start.19) | collective-permute-done | bytes 98336 | tf_op jit(solution)/shard_map/cond/branch_5_fun/ppermute | solution.py:367
  30.6 0.2 branch_5_fun.5
  30.8 3.9 %shard_map.139 = bf16[384,256]{1,0:T(8,128)(2,1)} custom-call(s32[2]{0:T(128)S(1)} %copy-done.7, f32[384,256]{1,0:T(8,128)S(1)} %get-tuple-element.146.stream_ref, bf16[8,48,768]{2,1,0:T(8,128)(2,1)S(1)} %get-tuple-element.150.held, bf16[8,48,512]{2,1,0:T(8,128)(2,1)S(1)} %get-tuple-element.151.beside, bf16[3,64,512]{2,1,0:T(8,128)(2,1)S(1)} %get-tuple-element.152.across, ...), custom_call_target="tpu_custom_call" | custom-call | tf_op jit(solution)/shard_map/pallas_call | solution.py:404
  (11 shorter events, 0.1 us)
Async XLA Ops:
  0.0 7.7 %copy-start.7 = (s32[2]{0:T(128)S(1)}, s32[2]{0:T(128)}, u32[]{:S(2)}) copy-start(s32[2]{0:T(128)} %place_ref.1) | copy-start | bytes 28
  0.0 9.0 %copy-start = (bf16[256,768]{1,0:T(8,128)(2,1)S(1)}, bf16[256,768]{1,0:T(8,128)(2,1)}, u32[]{:S(2)}) copy-start(bf16[256,768]{1,0:T(8,128)(2,1)} %refs_3_.3) | copy-start | bytes 1179652
  4.7 9.6 %copy-start.3 = (f32[384,256]{1,0:T(8,128)S(1)}, f32[384,256]{1,0:T(8,128)}, u32[]{:S(2)}) copy-start(f32[384,256]{1,0:T(8,128)} %get-tuple-element.139.stream_ref) | copy-start | bytes 1179652
  4.7 8.1 %collective-permute-start.28 = (bf16[384,256]{1,0:T(8,128)(2,1)}, bf16[384,256]{1,0:T(8,128)(2,1)S(1)}, u32[]{:S(2)}, u32[]{:S(2)}) collective-permute-start(bf16[384,256]{1,0:T(8,128)(2,1)} %get-tuple-element.140.refs_0_), channel_id=1, source_target_pairs={{0,16},{8,24},{16,0},{24,8},{1,17},{9,25},{17,1},{25,9},{2,18},{10... | collective-permute-start | bytes 589832 | tf_op jit(solution)/shard_map/ppermute | solution.py:301
  7.7 5.1 %collective-permute-start.29 = (bf16[384,256]{1,0:T(8,128)(2,1)}, bf16[384,256]{1,0:T(8,128)(2,1)S(1)}, u32[]{:S(2)}, u32[]{:S(2)}) collective-permute-start(bf16[384,256]{1,0:T(8,128)(2,1)} %get-tuple-element.140.refs_0_), channel_id=1, source_target_pairs={{0,8},{8,0},{16,24},{24,16},{1,9},{9,1},{17,25},{25,17},{2,10},{10... | collective-permute-start | bytes 589832 | tf_op jit(solution)/shard_map/ppermute | solution.py:307
  9.0 0.9 %copy-start.4 = (bf16[384,256]{1,0:T(8,128)(2,1)S(1)}, bf16[384,256]{1,0:T(8,128)(2,1)}, u32[]{:S(2)}) copy-start(bf16[384,256]{1,0:T(8,128)(2,1)} %get-tuple-element.140.refs_0_) | copy-start | bytes 589828
  9.9 4.3 %copy-start.5 = (bf16[256,256]{1,0:T(8,128)(2,1)S(1)}, bf16[256,256]{1,0:T(8,128)(2,1)}, u32[]{:S(2)}) copy-start(bf16[256,256]{1,0:T(8,128)(2,1)} %refs_4_.3) | copy-start | bytes 393220
  12.8 1.4 %collective-permute-start.30 = (bf16[384,256]{1,0:T(8,128)(2,1)S(1)}, bf16[384,256]{1,0:T(8,128)(2,1)S(1)}, u32[]{:S(2)}, u32[]{:S(2)}) collective-permute-start(bf16[384,256]{1,0:T(8,128)(2,1)S(1)} %collective-permute-done.28.refs_1_), channel_id=1, source_target_pairs={{0,8},{8,0},{16,24},{24,16},{1,9},{9,1},{17,25},{25,17},{2,10},{10... | collective-permute-start | bytes 589832 | tf_op jit(solution)/shard_map/ppermute | solution.py:327
  14.3 1.7 %copy-start.8 = (bf16[256,768]{1,0:T(8,128)(2,1)S(1)}, bf16[256,768]{1,0:T(8,128)(2,1)}, u32[]{:S(2)}) copy-start(bf16[256,768]{1,0:T(8,128)(2,1)} %param.31) | copy-start | bytes 1179652
  16.0 14.8 %copy-start.1 = (bf16[256,1024]{1,0:T(8,128)(2,1)S(1)}, bf16[256,1024]{1,0:T(8,128)(2,1)}, u32[]{:S(2)}) copy-start(bf16[256,1024]{1,0:T(8,128)(2,1)} %up_ref.1) | copy-start | bytes 1572868
  16.0 14.8 %copy-start.2 = (bf16[1024,256]{1,0:T(8,128)(2,1)S(1)}, bf16[1024,256]{1,0:T(8,128)(2,1)}, u32[]{:S(2)}) copy-start(bf16[1024,256]{1,0:T(8,128)(2,1)} %down_ref.1) | copy-start | bytes 1572868
  16.0 14.8 %copy-start.6 = (bf16[256,256]{1,0:T(8,128)(2,1)S(1)}, bf16[256,256]{1,0:T(8,128)(2,1)}, u32[]{:S(2)}) copy-start(bf16[256,256]{1,0:T(8,128)(2,1)} %out_ref.1) | copy-start | bytes 393220
  16.1 9.8 %collective-permute-start.17 = (bf16[6,48,256]{2,1,0:T(8,128)(2,1)S(1)}, bf16[6,48,256]{2,1,0:T(8,128)(2,1)S(1)}, u32[]{:S(2)}, u32[]{:S(2)}) collective-permute-start(bf16[6,48,256]{2,1,0:T(8,128)(2,1)S(1)} %slice.41), channel_id=1, source_target_pairs={{1,0},{2,1},{3,2},{0,3},{5,4},{6,5},{7,6},{4,7},{9,8},{10,9},{11,1... | collective-permute-start | bytes 442376 | tf_op jit(solution)/shard_map/cond/branch_5_fun/ppermute | solution.py:356
  20.0 5.9 %collective-permute-start.16 = (bf16[2,48,256]{2,1,0:T(8,128)(2,1)S(1)}, bf16[2,48,256]{2,1,0:T(8,128)(2,1)S(1)}, u32[]{:S(2)}, u32[]{:S(2)}) collective-permute-start(bf16[2,48,256]{2,1,0:T(8,128)(2,1)S(1)} %slice.40), channel_id=1, source_target_pairs={{0,1},{1,2},{2,3},{3,0},{4,5},{5,6},{6,7},{7,4},{8,9},{9,10},{10,1... | collective-permute-start | bytes 147464 | tf_op jit(solution)/shard_map/cond/branch_5_fun/ppermute | solution.py:355
  20.0 7.5 %collective-permute-start.18 = (bf16[192,256]{1,0:T(8,128)(2,1)S(1)}, bf16[192,256]{1,0:T(8,128)(2,1)S(1)}, u32[]{:S(2)}, u32[]{:S(2)}) collective-permute-start(bf16[192,256]{1,0:T(8,128)(2,1)S(1)} %get-tuple-element.109), channel_id=1, source_target_pairs={{0,4},{4,0},{1,5},{5,1},{2,6},{6,2},{3,7},{7,3},{8,12},{12,8},{9,1... | collective-permute-start | bytes 294920 | tf_op jit(solution)/shard_map/cond/branch_5_fun/ppermute | solution.py:357
  25.9 4.7 %collective-permute-start.19 = (bf16[192,256]{1,0:T(8,128)(2,1)S(1)}, bf16[192,256]{1,0:T(8,128)(2,1)S(1)}, u32[]{:S(2)}, u32[]{:S(2)}) collective-permute-start(bf16[192,256]{1,0:T(8,128)(2,1)S(1)} %get-tuple-element.114), channel_id=1, source_target_pairs={{0,4},{4,0},{1,5},{5,1},{2,6},{6,2},{3,7},{7,3},{8,12},{12,8},{9,1... | collective-permute-start | bytes 294920 | tf_op jit(solution)/shard_map/cond/branch_5_fun/ppermute | solution.py:367

commit v3 on v2

--- a/solution.py
+++ b/solution.py
@@ -33,7 +33,7 @@
     return lax.broadcasted_iota(jnp.int32, (1, channels), 1) // (channels // HEADS)
 
 
-def attend(query, key, value, bias):
+def partial_attention(query, key, value, bias):
     amount, channels = query.shape
     lanes = head_lanes(channels)
     scale = (channels // HEADS) ** (-0.5)
@@ -45,12 +45,26 @@
     top = jnp.max(scores, axis=-1, keepdims=True)
     powers = jnp.exp(scores - top)
     total = jnp.sum(powers, axis=-1, keepdims=True)
-    weights = (powers * (1.0 / total)).astype(bf16)
-    mixed = dot(weights.reshape(HEADS * amount, key.shape[0]), value)
-    result = mixed[:amount]
-    for head in range(1, HEADS):
-        result = jnp.where(lanes == head, mixed[head * amount : (head + 1) * amount], result)
-    return result.astype(bf16)
+    mixed = dot(powers.astype(bf16).reshape(HEADS * amount, key.shape[0]), value)
+
+    def in_lanes(parts):
+        result = parts[0]
+        for head in range(1, HEADS):
+            result = jnp.where(lanes == head, parts[head], result)
+        return jnp.broadcast_to(result, (amount, channels))
+
+    return in_lanes(mixed.reshape(HEADS, amount, channels)), in_lanes(top), in_lanes(total)
+
+
+def joined_attention(one, two):
+    top = jnp.maximum(one[1], two[1])
+    first, second = jnp.exp(one[1] - top), jnp.exp(two[1] - top)
+    return (first * one[0] + second * two[0]) / (first * one[2] + second * two[2])
+
+
+def attend(query, key, value, bias):
+    mixed, _, total = partial_attention(query, key, value, bias)
+    return (mixed / total).astype(bf16)
 
 
 def feed_forward(stream, up_ref, down_ref, chunk=256):
@@ -116,37 +130,47 @@
     normed_ref[...] = normalize(stream)
 
 
+def member_pairs(shape, block_refs, qkv_ref, pairs):
+    members, height, breadth, channels = shape
+    rows = members * height
+    for index, block_ref in enumerate(block_refs):
+        pairs[:, index * rows : (index + 1) * rows, :] = (
+            dot(block_ref[...], qkv_ref[:, channels:]).astype(bf16).reshape(breadth, rows, 2 * channels)
+        )
+    amount = pairs.shape[1]
+    row = lax.broadcasted_iota(jnp.int32, (rows, amount), 0) % height
+    other = lax.broadcasted_iota(jnp.int32, (rows, amount), 1) % height
+    return jnp.where(row == other, 0.0, MASKED).astype(f32)
+
+
 def near_kernel(shape, *refs):
     members, height, breadth, channels = shape
-    *block_refs, qkv_ref, queries_ref, pairs_ref = refs
+    *block_refs, qkv_ref, queries_ref, mixed_ref, top_ref, total_ref, pairs = refs
     rows = members * height
     queries_ref[...] = (
         dot(block_refs[0][...], qkv_ref[:, :channels]).astype(bf16).reshape(breadth, rows, channels)
     )
-    for index, block_ref in enumerate(block_refs):
-        pairs_ref[:, index * rows : (index + 1) * rows, :] = (
-            dot(block_ref[...], qkv_ref[:, channels:]).astype(bf16).reshape(breadth, rows, 2 * channels)
-        )
-
-
-def member_kernel(shape, lat_count, stream_ref, queries_ref, pairs_ref, *refs):
+    bias = member_pairs(shape, block_refs, qkv_ref, pairs)
+    for column in range(breadth):
+        mixed_ref[column], top_ref[column], total_ref[column] = partial_attention(
+            queries_ref[column], pairs[column, :, :channels], pairs[column, :, channels:], bias
+        )
+
+
+def member_kernel(shape, lat_count, stream_ref, queries_ref, mixed_ref, top_ref, total_ref, *refs):
     members, height, breadth, channels = shape
     sides = 1 if lat_count == 2 else 2
     *block_refs, qkv_ref, out_ref = refs[: -4 - sides]
     late_ref, normed_ref, *edge_refs = refs[-4 - sides : -2]
-    far, attended = refs[-2:]
+    pairs, attended = refs[-2:]
     rows = members * height
-    amount = rows * len(block_refs) + pairs_ref.shape[1]
-    for index, block_ref in enumerate(block_refs):
-        far[:, index * rows : (index + 1) * rows, :] = (
-            dot(block_ref[...], qkv_ref[:, channels:]).astype(bf16).reshape(breadth, rows, 2 * channels)
-        )
-    row = lax.broadcasted_iota(jnp.int32, (rows, amount), 0) % height
-    other = lax.broadcasted_iota(jnp.int32, (rows, amount), 1) % height
-    bias = jnp.where(row == other, 0.0, MASKED).astype(f32)
+    bias = member_pairs(shape, block_refs, qkv_ref, pairs)
     for column in range(breadth):
-        both = jnp.concatenate([pairs_ref[column], far[column]], axis=0)
-        attended[column] = attend(queries_ref[column], both[:, :channels], both[:, channels:], bias)
+        far = partial_attention(
+            queries_ref[column], pairs[column, :, :channels], pairs[column, :, channels:], bias
+        )
+        near = mixed_ref[column], top_ref[column], total_ref[column]
+        attended[column] = joined_attention(near, far).astype(bf16)
     stream = stream_ref[...] + dot(attended[...].reshape(breadth * rows, channels), out_ref[...])
     late_ref[...] = stream
     normed = normalize(stream)
@@ -184,16 +208,58 @@
     return [bottom, top]
 
 
-def early_kernel(shape, normed_ref, side_ref, edge_ref, qkv_ref, held_ref, beside_ref, across_ref):
-    members, height, breadth, channels = shape
-    rows = members * height
-    held_ref[...] = dot(normed_ref[...], qkv_ref[...]).astype(bf16).reshape(breadth, rows, 3 * channels)
-    beside_ref[...] = dot(side_ref[...], qkv_ref[:, channels:]).astype(bf16).reshape(
+def lat_window(row, place_ref):
+    return (row - place_ref[:, :1] + WIN) // WIN
+
+
+def shifted_bias(shape, place_ref, key_lat, key_lon):
+    members, height, breadth, channels = shape
+    index = lax.broadcasted_iota(jnp.int32, (breadth * height, 1), 0)
+    query_lon = jnp.where(index // height >= place_ref[:, 1:], 1, 0)
+    query_tag = 2 * lat_window(index % height, place_ref) + query_lon
+    return jnp.where(query_tag == 2 * key_lat + key_lon, 0.0, MASKED).astype(f32)
+
+
+def early_kernel(
+    shape, lat_count, place_ref, normed_ref, side_ref, edge_ref, qkv_ref,
+    queries_ref, mixed_ref, top_ref, total_ref, across_ref, late_bias_ref, held, beside,
+):
+    members, height, breadth, channels = shape
+    rows, tokens = members * height, breadth * height
+    held[...] = dot(normed_ref[...], qkv_ref[...]).astype(bf16).reshape(breadth, rows, 3 * channels)
+    beside[...] = dot(side_ref[...], qkv_ref[:, channels:]).astype(bf16).reshape(
         breadth, rows, 2 * channels
     )
     edge = per_member(dot(edge_ref[...], qkv_ref[:, channels:]), members, breadth)
+    index = lax.broadcasted_iota(jnp.int32, (1, 2 * tokens), 1)
+    mixed, local = index // tokens, index % tokens
+    key_lon = jnp.where(local // height >= place_ref[:, 1:], 1 - mixed, mixed)
+    bias = shifted_bias(shape, place_ref, lat_window(local % height, place_ref), key_lon)
     for member in range(members):
         across_ref[member] = edge[member]
+        part = slice(member * height, (member + 1) * height)
+        query = held[:, part, :channels].reshape(tokens, channels)
+        queries_ref[member] = query
+        key, value = (
+            jnp.concatenate(
+                [
+                    held[:, part, (i + 1) * channels : (i + 2) * channels].reshape(tokens, channels),
+                    beside[:, part, i * channels : (i + 1) * channels].reshape(tokens, channels),
+                ],
+                axis=0,
+            )
+            for i in range(2)
+        )
+        mixed_ref[member], top_ref[member], total_ref[member] = partial_attention(query, key, value, bias)
+
+    edge_tokens = breadth * WIN
+    first = jnp.where(lax.axis_index("lat") == 0, 1, 0)
+    last = jnp.where(lax.axis_index("lat") == lat_count - 1, 1, 0)
+    index = lax.broadcasted_iota(jnp.int32, (1, 2 * edge_tokens), 1)
+    mixed, local = index // edge_tokens, index % edge_tokens
+    key_lat = jnp.where(local % WIN >= place_ref[:, :1], -1000 * first, height // WIN - 1000 * last)
+    key_lon = jnp.where(local // WIN >= place_ref[:, 1:], 1 - mixed, mixed)
+    late_bias_ref[...] = shifted_bias(shape, place_ref, key_lat, key_lon)
 
 
 def corner_kernel(shape, corner_ref, qkv_ref, corner_pairs_ref):
@@ -204,49 +270,24 @@
 
 
 def shift_kernel(
-    shape, lat_count, place_ref, stream_ref, held, beside, across, corner, out_ref, up_ref, down_ref,
-    updated_ref, attended, turned,
+    shape, stream_ref, queries_ref, mixed_ref, top_ref, total_ref, across, bias_ref, corner, out_ref, up_ref,
+    down_ref, updated_ref, attended, turned,
 ):
     members, height, breadth, channels = shape
     rows = members * height
-    tokens, edge_tokens = breadth * height, breadth * WIN
-
-    lat_shift, lon_shift = place_ref[0], place_ref[1]
-    first = jnp.where(lax.axis_index("lat") == 0, 1, 0)
-    last = jnp.where(lax.axis_index("lat") == lat_count - 1, 1, 0)
-    amount = 2 * tokens + 2 * edge_tokens
-    query_index = lax.broadcasted_iota(jnp.int32, (tokens, 1), 0)
-    query_row, query_column = query_index % height, query_index // height
-    query_tag = 2 * ((query_row - lat_shift + WIN) // WIN) + jnp.where(query_column >= lon_shift, 1, 0)
-    index = lax.broadcasted_iota(jnp.int32, (1, amount), 1)
-    whole = index < 2 * tokens
-    local = jnp.where(whole, index % tokens, (index - 2 * tokens) % edge_tokens)
-    mixed = jnp.where(whole, index // tokens, jnp.where(index < 2 * tokens + edge_tokens, 0, 1))
-    key_row = jnp.where(whole, local % height, local % WIN)
-    key_column = jnp.where(whole, local // height, local // WIN)
-    edge_lat = jnp.where(key_row >= lat_shift, -1000 * first, height // WIN - 1000 * last)
-    key_lat = jnp.where(whole, (key_row - lat_shift + WIN) // WIN, edge_lat)
-    key_lon = jnp.where(key_column >= lon_shift, 1 - mixed, mixed)
-    bias = jnp.where(query_tag == 2 * key_lat + key_lon, 0.0, MASKED).astype(f32)
-
+    bias = bias_ref[...]
     for member in range(members):
-        part = slice(member * height, (member + 1) * height)
-        query = held[:, part, :channels].reshape(tokens, channels)
-        pairs = []
-        for i in range(2):
-            lanes = slice(i * channels, (i + 1) * channels)
-            pairs.append(
-                jnp.concatenate(
-                    [
-                        held[:, part, (i + 1) * channels : (i + 2) * channels].reshape(tokens, channels),
-                        beside[:, part, lanes].reshape(tokens, channels),
-                        across[member, :, lanes],
-                        corner[member, :, lanes],
-                    ],
-                    axis=0,
-                )
+        key, value = (
+            jnp.concatenate(
+                [block[member, :, i * channels : (i + 1) * channels] for block in (across, corner)], axis=0
             )
-        attended[:, part, :] = attend(query, pairs[0], pairs[1], bias).reshape(breadth, height, channels)
+            for i in range(2)
+        )
+        late = partial_attention(queries_ref[member], key, value, bias)
+        early = mixed_ref[member], top_ref[member], total_ref[member]
+        attended[:, member * height : (member + 1) * height, :] = (
+            joined_attention(early, late).astype(bf16).reshape(breadth, height, channels)
+        )
     stream = stream_ref[...] + dot(attended[...].reshape(breadth * rows, channels), out_ref[...])
     stream = feed_forward(stream, up_ref, down_ref)
     for column in range(breadth):
@@ -299,33 +340,29 @@
     while bit * 2 < groups:
         bit *= 2
     far = [lax.ppermute(normed, "member", [(i, i ^ bit) for i in range(groups)])]
-    near = []
     partners = []
     while bit > 1:
         bit //= 2
         partners.append([(i, i ^ bit) for i in range(groups)])
-        near = near + [lax.ppermute(block, "member", partners[-1]) for block in blocks + near]
-
-    queries, pairs = pl.pallas_call(
+
+    def spread(blocks):
+        for partner in partners:
+            blocks = blocks + [lax.ppermute(block, "member", partner) for block in blocks]
+        return blocks
+
+    near = spread([normed])
+    part_shape = jax.ShapeDtypeStruct((breadth, rows, channels), f32)
+    queries, *parts = pl.pallas_call(
         functools.partial(near_kernel, shape),
-        out_shape=(
-            jax.ShapeDtypeStruct((breadth, rows, channels), bf16),
-            jax.ShapeDtypeStruct((breadth, rows * len(blocks), 2 * channels), bf16),
-        ),
-        in_specs=in_vmem(1 + len(blocks)),
-        out_specs=tuple(in_vmem(2)),
+        out_shape=(jax.ShapeDtypeStruct((breadth, rows, channels), bf16),) + (part_shape,) * 3,
+        in_specs=in_vmem(1 + len(near)),
+        out_specs=tuple(in_vmem(4)),
+        scratch_shapes=[pltpu.VMEM((breadth, rows * len(near), 2 * channels), bf16)],
         compiler_params=params,
-        cost_estimate=pl.CostEstimate(
-            flops=2 * tokens * channels * channels * (1 + 2 * len(blocks)),
-            bytes_accessed=2 * tokens * channels * 6,
-            transcendentals=0,
-        ),
-    )(*blocks, mem_qkv)
+    )(*near, mem_qkv)
     branch = offsets[1] - 1
-    far[0], branch, queries, pairs = lax.optimization_barrier((far[0], branch, queries, pairs))
-    for partner in partners:
-        far = far + [lax.ppermute(block, "member", partner) for block in far]
-    far = near + far
+    far[0], branch, queries, *parts = lax.optimization_barrier((far[0], branch, queries, *parts))
+    far = spread(far)
 
     lat_count, lon_count = lax.axis_size("lat"), lax.axis_size("lon")
     lat_index = lax.axis_index("lat")
@@ -339,14 +376,14 @@
             jax.ShapeDtypeStruct((tokens, channels), bf16),
         )
         + (jax.ShapeDtypeStruct((edge_tokens, channels), bf16),) * len(lat_pairs),
-        in_specs=in_vmem(5 + len(far)),
+        in_specs=in_vmem(7 + len(far)),
         out_specs=tuple(in_vmem(2 + len(lat_pairs))),
         scratch_shapes=[
             pltpu.VMEM((breadth, rows * len(far), 2 * channels), bf16),
             pltpu.VMEM((breadth, rows, channels), bf16),
         ],
         compiler_params=params,
-    )(stream, queries, pairs, *far, mem_qkv, mem_out)
+    )(stream, queries, *parts, *far, mem_qkv, mem_out)
 
     ring = [(i, (i + 1) % lon_count) for i in range(lon_count)]
     back = [(b, a) for a, b in ring]
@@ -379,41 +416,40 @@
             out_specs=in_vmem(1)[0],
             compiler_params=params,
         )(corner, shift_qkv)
+        bias_shape = jax.ShapeDtypeStruct((breadth * height, 2 * breadth * WIN), f32)
+        whole_shape = (members, breadth * height, channels)
         return pl.pallas_call(
-            functools.partial(early_kernel, shape),
-            out_shape=(
-                jax.ShapeDtypeStruct((breadth, rows, 3 * channels), bf16),
-                jax.ShapeDtypeStruct((breadth, rows, 2 * channels), bf16),
-                pairs_shape,
-            ),
-            in_specs=in_vmem(4),
-            out_specs=tuple(in_vmem(3)),
+            functools.partial(early_kernel, shape, lat_count),
+            out_shape=(jax.ShapeDtypeStruct(whole_shape, bf16),)
+            + (jax.ShapeDtypeStruct(whole_shape, f32),) * 3
+            + (pairs_shape, bias_shape),
+            in_specs=in_vmem(5),
+            out_specs=tuple(in_vmem(6)),
+            scratch_shapes=[
+                pltpu.VMEM((breadth, rows, 3 * channels), bf16),
+                pltpu.VMEM((breadth, rows, 2 * channels), bf16),
+            ],
             compiler_params=params,
-            cost_estimate=pl.CostEstimate(
-                flops=2 * tokens * channels * channels * 6,
-                bytes_accessed=2 * tokens * channels * 8,
-                transcendentals=0,
-            ),
-        )(own.reshape(tokens, channels), side.reshape(tokens, channels), edge, shift_qkv) + (corner,)
-
-    held, beside, across, corner = lax.switch(
+        )(offsets.reshape(1, -1), own.reshape(tokens, channels), side.reshape(tokens, channels), edge, shift_qkv) + (
+            corner,
+        )
+
+    *early, corner = lax.switch(
         branch,
         [functools.partial(gather, amount) for amount in range(1, WIN)],
         normed.reshape(breadth, rows, channels), *edges,
     )
     updated = pl.pallas_call(
-        functools.partial(shift_kernel, shape, lat_count),
+        functools.partial(shift_kernel, shape),
         out_shape=jax.ShapeDtypeStruct((tokens, channels), bf16),
-        in_specs=[pl.BlockSpec(memory_space=pltpu.SMEM)] + in_vmem(8),
+        in_specs=in_vmem(11),
         out_specs=pl.BlockSpec(memory_space=pltpu.VMEM),
         scratch_shapes=[
             pltpu.VMEM((breadth, rows, channels), bf16),
             pltpu.VMEM((channels // LANES, tokens, LANES), f32),
         ],
         compiler_params=params,
-    )(
-        offsets, late, held, beside, across, corner, shift_out, shift_up, shift_down,
-    )
+    )(late, *early, corner, shift_out, shift_up, shift_down)
     return updated.reshape(shape)
 
 

time: 34.3 us -> 32.6 us (0.950); the launches traced: 34.7 us -> 32.4 us
  waiting for transfers between devices: 11 us -> 8.66 us
  Pallas kernels: 11.3 us -> 10.8 us
    ppermute x1, waiting for transfers between devices: 4.33 us -> 0.01 us  [gather(): low = lax.ppermute(own[amount:], 'lon', ring)]
    ppermute x1, waiting for transfers between devices: 0.01 us -> 2.95 us  [gather(): high = lax.ppermute(own[:amount], 'lon', back)]
    ppermute x1, starting transfers between devices: 0.01 us -> 1.87 us  [gather(): low = lax.ppermute(own[amount:], 'lon', ring)]
    ppermute x1, starting transfers between devices: 3.87 us -> 2.1 us  [gather(): high = lax.ppermute(own[:amount], 'lon', back)]
    pallas_call x1, Pallas kernels: 0.31 us -> 1.08 us  [per_device(): pl.pallas_call(functools.partial(near_kernel, shape), out_shape=(jax.Shap...]
    ppermute x1, waiting for transfers between devices: 2.64 us -> 1.88 us  [gather(): lax.ppermute(end, 'lat', pairs)]
    pallas_call x2, Pallas kernels: 4.39 us -> 3.87 us  [the longest x1 2.69 us: per_device(): pl.pallas_call(functools.partial(shift_kernel, shape), out_shape=jax.Shap...]
    ppermute x2, starting transfers between devices: 0.01 us -> 0.52 us  [spread(): lax.ppermute(block, 'member', partner)]
  transfers between devices with their start and end apart: 7 -> 7, of which waited for: 4 -> 4; matrix products, arithmetic and copies ran while one was open for 2% -> 2% of each run, Pallas kernels for 2% -> 7%
where the time goes in v3:
time: 32.6 us; the launch traced here: 32.4 us
  Pallas kernels  10.8 us (33%)
  starting transfers between devices  10.3 us (32%)
  waiting for transfers between devices  8.66 us (27%)
  local copies, waits for them, and re-layouts  1.62 us (5%)
  between operations  0.76 us (2%)
    pallas_call x1, Pallas kernels, per_device(): pl.pallas_call(functools.partial(window_kernel, shape), out_shape=(jax.Sh...  4.23 us
    ppermute x1, waiting for transfers between devices, gather(): high = lax.ppermute(own[:amount], 'lon', back)  2.95 us
    pallas_call x1, Pallas kernels, per_device(): pl.pallas_call(functools.partial(shift_kernel, shape), out_shape=jax.Shap...  2.69 us
    ppermute x1, starting transfers between devices, per_device(): lax.ppermute(normed, 'member', [(i, i ^ bit) for i in range(groups)])  2.59 us
    ppermute x1, waiting for transfers between devices, per_device(): lax.ppermute(normed, 'member', [(i, i ^ bit) for i in range(groups)])  2.38 us
    ppermute x1, starting transfers between devices, gather(): high = lax.ppermute(own[:amount], 'lon', back)  2.1 us
    ppermute x1, waiting for transfers between devices, gather(): lax.ppermute(end, 'lat', pairs)  1.88 us
    ppermute x1, starting transfers between devices, gather(): low = lax.ppermute(own[amount:], 'lon', ring)  1.87 us
  transfers between devices with their start and end apart: 7, of which 4 were waited for; matrix products, arithmetic and copies ran while one was open for 2% of the time, Pallas kernels for 7%

profile of v3, /device:TPU:0, one launch (start us, length us, event | category | flops | bytes accessed | tf_op | source)
XLA Modules:
  0.0 32.4 jit_solution(14183822823037677661)
XLA Ops:
  0.0 4.2 %shard_map.136 = (f32[384,256]{1,0:T(8,128)}, bf16[384,256]{1,0:T(8,128)(2,1)}) custom-call(bf16[384,256]{1,0:T(8,128)(2,1)} %bitcast.47, s32[8,16]{1,0:T(8,128)} %bitcast.55, f32[1,256]{1,0:T(1,128)} %bitcast.56, bf16[256,768]{1,0:T(8,128)(2,1)} %refs_3_.2, bf16[256,256]{1,0:T(8,128)(2,1)} %refs_4_.1, bf16[256,1024]{1,0:T(8,128)(2,1)} %refs_5_.1, ...), custom_call_target="tpu_custom_call" | custom-call | tf_op jit(solution)/shard_map/pallas_call | solution.py:319
  4.2 0.0 copy-start.8
  4.3 0.5 %collective-permute-start.29 = (bf16[384,256]{1,0:T(8,128)(2,1)}, bf16[384,256]{1,0:T(8,128)(2,1)S(1)}, u32[]{:S(2)}, u32[]{:S(2)}) collective-permute-start(bf16[384,256]{1,0:T(8,128)(2,1)} %get-tuple-element.189.refs_0_), channel_id=1, source_target_pairs={{0,8},{8,0},{16,24},{24,16},{1,9},{9,1},{17,25},{25,17},{2,10},{10... | collective-permute-start | bytes 589832 | tf_op jit(solution)/shard_map/ppermute | solution.py:350
  4.8 2.6 %collective-permute-start.28 = (bf16[384,256]{1,0:T(8,128)(2,1)}, bf16[384,256]{1,0:T(8,128)(2,1)S(1)}, u32[]{:S(2)}, u32[]{:S(2)}) collective-permute-start(bf16[384,256]{1,0:T(8,128)(2,1)} %get-tuple-element.189.refs_0_), channel_id=1, source_target_pairs={{0,16},{8,24},{16,0},{24,8},{1,17},{9,25},{17,1},{25,9},{2,18},{10... | collective-permute-start | bytes 589832 | tf_op jit(solution)/shard_map/ppermute | solution.py:342
  7.4 0.0 copy-done.8
  7.4 0.6 %slice.45 = s32[1]{0:T(128)} slice(s32[2]{0:T(128)S(1)} %copy-done.8), slice={[1:2]} | slice | bytes 8 | tf_op jit(solution)/shard_map/slice | solution.py:363
  8.6 0.0 copy-start.3
  8.6 0.0 collective-permute-done.29.refs_1_
  8.6 0.0 copy-done
  8.6 0.0 copy-start.4
  8.6 1.0 %copy-done.4 = bf16[384,256]{1,0:T(8,128)(2,1)S(1)} copy-done((bf16[384,256]{1,0:T(8,128)(2,1)S(1)}, bf16[384,256]{1,0:T(8,128)(2,1)}, u32[]{:S(2)}) %copy-start.4) | copy-done | bytes 196632
  9.6 1.1 %shard_map.137 = (bf16[8,48,256]{2,1,0:T(8,128)(2,1)S(1)}, f32[8,48,256]{2,1,0:T(8,128)S(1)}, f32[8,48,256]{2,1,0:T(8,128)S(1)}, f32[8,48,256]{2,1,0:T(8,128)S(1)}) custom-call(bf16[384,256]{1,0:T(8,128)(2,1)S(1)} %copy-done.4, bf16[384,256]{1,0:T(8,128)(2,1)S(1)} %collective-permute-done.29.refs_1_, bf16[256,768]{1,0:T(8,128)(2,1)S(1)} %copy-done), custom_call_target="tpu_custom_call" | custom-call | tf_op jit(solution)/shard_map/pallas_call | solution.py:355
  10.7 2.4 %collective-permute-done.28.refs_0_ = bf16[384,256]{1,0:T(8,128)(2,1)S(1)} collective-permute-done((bf16[384,256]{1,0:T(8,128)(2,1)}, bf16[384,256]{1,0:T(8,128)(2,1)S(1)}, u32[]{:S(2)}, u32[]{:S(2)}) %collective-permute-start.28) | collective-permute-done | bytes 196640 | tf_op jit(solution)/shard_map/ppermute | solution.py:342
  13.1 0.0 collective-permute-start.30
  13.1 1.4 %collective-permute-done.30.refs_1_ = bf16[384,256]{1,0:T(8,128)(2,1)S(1)} collective-permute-done((bf16[384,256]{1,0:T(8,128)(2,1)S(1)}, bf16[384,256]{1,0:T(8,128)(2,1)S(1)}, u32[]{:S(2)}, u32[]{:S(2)}) %collective-permute-start.30) | collective-permute-done | bytes 196640 | tf_op jit(solution)/shard_map/ppermute | solution.py:350
  14.5 0.0 copy-done.3
  14.5 1.3 %shard_map.138 = (f32[384,256]{1,0:T(8,128)S(1)}, bf16[384,256]{1,0:T(8,128)(2,1)S(1)}, bf16[192,256]{1,0:T(8,128)(2,1)S(1)}) custom-call(f32[384,256]{1,0:T(8,128)S(1)} %copy-done.3, bf16[8,48,256]{2,1,0:T(8,128)(2,1)S(1)} %get-tuple-element.194.queries_ref, f32[8,48,256]{2,1,0:T(8,128)S(1)} %get-tuple-element.195.mixed_ref, ...), custom_call_target="tpu_custom_call" | custom-call | tf_op jit(solution)/shard_map/pallas_call | solution.py:372
  15.9 0.0 copy-start.1
  15.9 0.0 copy-start.2
  15.9 0.0 copy-start.5
  15.9 13.8 %conditional.1 = (bf16[3,128,256]{2,1,0:T(8,128)(2,1)S(1)}, f32[3,128,256]{2,1,0:T(8,128)S(1)}, f32[3,128,256]{2,1,0:T(8,128)S(1)}, f32[3,128,256]{2,1,0:T(8,128...) conditional(s32[]{:T(128)} %clamp.3, (s32[2]{0:T(128)S(1)}, ...), branch_computations={%region_0.0_spmd, %region_1.0_spmd, %region_2.0_spmd, %region_3.0_... | conditional | bytes 1966296 | solution.py:437
  16.0 1.9 %collective-permute-start.5 = (bf16[6,48,256]{2,1,0:T(8,128)(2,1)S(1)}, bf16[6,48,256]{2,1,0:T(8,128)(2,1)S(1)}, u32[]{:S(2)}, u32[]{:S(2)}) collective-permute-start(bf16[6,48,256]{2,1,0:T(8,128)(2,1)S(1)} %slice.33), channel_id=1, source_target_pairs={{0,1},{1,2},{2,3},{3,0},{4,5},{5,6},{6,7},{7,4},{8,9},{9,10},{10,1... | collective-permute-start | bytes 442376 | tf_op jit(solution)/shard_map/cond/branch_1_fun/ppermute | solution.py:392
  17.8 2.1 %collective-permute-start.4 = (bf16[2,48,256]{2,1,0:T(8,128)(2,1)S(1)}, bf16[2,48,256]{2,1,0:T(8,128)(2,1)S(1)}, u32[]{:S(2)}, u32[]{:S(2)}) collective-permute-start(bf16[2,48,256]{2,1,0:T(8,128)(2,1)S(1)} %slice.32), channel_id=1, source_target_pairs={{1,0},{2,1},{3,2},{0,3},{5,4},{6,5},{7,6},{4,7},{9,8},{10,9},{11,1... | collective-permute-start | bytes 147464 | tf_op jit(solution)/shard_map/cond/branch_1_fun/ppermute | solution.py:393
  19.9 1.6 %collective-permute-start.6 = (bf16[192,256]{1,0:T(8,128)(2,1)S(1)}, bf16[192,256]{1,0:T(8,128)(2,1)S(1)}, u32[]{:S(2)}, u32[]{:S(2)}) collective-permute-start(bf16[192,256]{1,0:T(8,128)(2,1)S(1)} %get-tuple-element.92), channel_id=1, source_target_pairs={{0,4},{4,0},{1,5},{5,1},{2,6},{6,2},{3,7},{7,3},{8,12},{12,8},{9,1... | collective-permute-start | bytes 294920 | tf_op jit(solution)/shard_map/cond/branch_1_fun/ppermute | solution.py:394
  21.6 3.0 %collective-permute-done.4.first_ref = bf16[2,48,256]{2,1,0:T(8,128)(2,1)S(1)} collective-permute-done((bf16[2,48,256]{2,1,0:T(8,128)(2,1)S(1)}, bf16[2,48,256]{2,1,0:T(8,128)(2,1)S(1)}, u32[]{:S(2)}, u32[]{:S(2)}) %collective-permute-start.4) | collective-permute-done | bytes 49184 | tf_op jit(solution)/shard_map/cond/branch_1_fun/ppermute | solution.py:393
  24.5 0.0 collective-permute-done.5.second_ref
  24.6 1.6 %collective-permute-start.7 = (bf16[192,256]{1,0:T(8,128)(2,1)S(1)}, bf16[192,256]{1,0:T(8,128)(2,1)S(1)}, u32[]{:S(2)}, u32[]{:S(2)}) collective-permute-start(bf16[192,256]{1,0:T(8,128)(2,1)S(1)} %get-tuple-element.100), channel_id=1, source_target_pairs={{0,4},{4,0},{1,5},{5,1},{2,6},{6,2},{3,7},{7,3},{8,12},{12,8},{9,1... | collective-permute-start | bytes 294920 | tf_op jit(solution)/shard_map/cond/branch_1_fun/ppermute | solution.py:404
  26.2 0.0 collective-permute-done.6.edge_ref
  26.2 1.2 %branch_1_fun.4 = (bf16[3,128,256]{2,1,0:T(8,128)(2,1)S(1)}, f32[3,128,256]{2,1,0:T(8,128)S(1)}, f32[3,128,256]{2,1,0:T(8,128)S(1)}, f32[3,128,256]{2,1,0:T(8,12...) custom-call(s32[1,2]{1,0:T(1,128)S(1)} %bitcast.49, bf16[384,256]{1,0:T(8,128)(2,1)S(1)} %get-tuple-element.89.normed_ref, ...), custom_call_target="tpu_custom_call" | custom-call | tf_op jit(solution)/shard_map/cond/branch_1_fun/pallas_call | solution.py:421
  27.4 1.9 %collective-permute-done.7.corner_ref = bf16[192,256]{1,0:T(8,128)(2,1)S(1)} collective-permute-done((bf16[192,256]{1,0:T(8,128)(2,1)S(1)}, bf16[192,256]{1,0:T(8,128)(2,1)S(1)}, u32[]{:S(2)}, u32[]{:S(2)}) %collective-permute-start.7) | collective-permute-done | bytes 98336 | tf_op jit(solution)/shard_map/cond/branch_1_fun/ppermute | solution.py:404
  29.3 0.2 branch_1_fun.5
  29.7 2.7 %shard_map.139 = bf16[384,256]{1,0:T(8,128)(2,1)} custom-call(f32[384,256]{1,0:T(8,128)S(1)} %get-tuple-element.199.stream_ref, bf16[3,128,256]{2,1,0:T(8,128)(2,1)S(1)} %get-tuple-element.203.queries_ref, f32[3,128,256]{2,1,0:T(8,128)S(1)} %get-tuple-element.204.mixed_ref, f32[3,128,256]{2,1,0:T(8,128)S(1)} %get-tuple-element.205.top_ref, ...), custom_call_target="tpu_custom_call" | custom-call | tf_op jit(solution)/shard_map/pallas_call | solution.py:442
  (11 shorter events, 0.1 us)
Async XLA Ops:
  0.0 8.6 %copy-start = (bf16[256,768]{1,0:T(8,128)(2,1)S(1)}, bf16[256,768]{1,0:T(8,128)(2,1)}, u32[]{:S(2)}) copy-start(bf16[256,768]{1,0:T(8,128)(2,1)} %refs_2_.3) | copy-start | bytes 1179652
  4.2 3.1 %copy-start.8 = (s32[2]{0:T(128)S(1)}, s32[2]{0:T(128)}, u32[]{:S(2)}) copy-start(s32[2]{0:T(128)} %param.23) | copy-start | bytes 28
  4.3 4.3 %collective-permute-start.29 = (bf16[384,256]{1,0:T(8,128)(2,1)}, bf16[384,256]{1,0:T(8,128)(2,1)S(1)}, u32[]{:S(2)}, u32[]{:S(2)}) collective-permute-start(bf16[384,256]{1,0:T(8,128)(2,1)} %get-tuple-element.189.refs_0_), channel_id=1, source_target_pairs={{0,8},{8,0},{16,24},{24,16},{1,9},{9,1},{17,25},{25,17},{2,10},{10... | collective-permute-start | bytes 589832 | tf_op jit(solution)/shard_map/ppermute | solution.py:350
  4.8 8.3 %collective-permute-start.28 = (bf16[384,256]{1,0:T(8,128)(2,1)}, bf16[384,256]{1,0:T(8,128)(2,1)S(1)}, u32[]{:S(2)}, u32[]{:S(2)}) collective-permute-start(bf16[384,256]{1,0:T(8,128)(2,1)} %get-tuple-element.189.refs_0_), channel_id=1, source_target_pairs={{0,16},{8,24},{16,0},{24,8},{1,17},{9,25},{17,1},{25,9},{2,18},{10... | collective-permute-start | bytes 589832 | tf_op jit(solution)/shard_map/ppermute | solution.py:342
  8.6 5.9 %copy-start.3 = (f32[384,256]{1,0:T(8,128)S(1)}, f32[384,256]{1,0:T(8,128)}, u32[]{:S(2)}) copy-start(f32[384,256]{1,0:T(8,128)} %get-tuple-element.188.stream_ref) | copy-start | bytes 1179652
  8.6 1.0 %copy-start.4 = (bf16[384,256]{1,0:T(8,128)(2,1)S(1)}, bf16[384,256]{1,0:T(8,128)(2,1)}, u32[]{:S(2)}) copy-start(bf16[384,256]{1,0:T(8,128)(2,1)} %get-tuple-element.189.refs_0_) | copy-start | bytes 589828
  9.6 4.9 %copy-start.6 = (bf16[256,256]{1,0:T(8,128)(2,1)S(1)}, bf16[256,256]{1,0:T(8,128)(2,1)}, u32[]{:S(2)}) copy-start(bf16[256,256]{1,0:T(8,128)(2,1)} %refs_3_.3) | copy-start | bytes 393220
  13.1 1.4 %collective-permute-start.30 = (bf16[384,256]{1,0:T(8,128)(2,1)S(1)}, bf16[384,256]{1,0:T(8,128)(2,1)S(1)}, u32[]{:S(2)}, u32[]{:S(2)}) collective-permute-start(bf16[384,256]{1,0:T(8,128)(2,1)S(1)} %collective-permute-done.28.refs_0_), channel_id=1, source_target_pairs={{0,8},{8,0},{16,24},{24,16},{1,9},{9,1},{17,25},{25,17},{2,10},{10... | collective-permute-start | bytes 589832 | tf_op jit(solution)/shard_map/ppermute | solution.py:350
  14.5 1.3 %copy-start.7 = (bf16[256,768]{1,0:T(8,128)(2,1)S(1)}, bf16[256,768]{1,0:T(8,128)(2,1)}, u32[]{:S(2)}) copy-start(bf16[256,768]{1,0:T(8,128)(2,1)} %param.31) | copy-start | bytes 1179652
  15.9 13.8 %copy-start.1 = (bf16[256,1024]{1,0:T(8,128)(2,1)S(1)}, bf16[256,1024]{1,0:T(8,128)(2,1)}, u32[]{:S(2)}) copy-start(bf16[256,1024]{1,0:T(8,128)(2,1)} %up_ref.1) | copy-start | bytes 1572868
  15.9 13.8 %copy-start.2 = (bf16[1024,256]{1,0:T(8,128)(2,1)S(1)}, bf16[1024,256]{1,0:T(8,128)(2,1)}, u32[]{:S(2)}) copy-start(bf16[1024,256]{1,0:T(8,128)(2,1)} %down_ref.1) | copy-start | bytes 1572868
  15.9 13.8 %copy-start.5 = (bf16[256,256]{1,0:T(8,128)(2,1)S(1)}, bf16[256,256]{1,0:T(8,128)(2,1)}, u32[]{:S(2)}) copy-start(bf16[256,256]{1,0:T(8,128)(2,1)} %out_ref.1) | copy-start | bytes 393220
  16.0 8.6 %collective-permute-start.5 = (bf16[6,48,256]{2,1,0:T(8,128)(2,1)S(1)}, bf16[6,48,256]{2,1,0:T(8,128)(2,1)S(1)}, u32[]{:S(2)}, u32[]{:S(2)}) collective-permute-start(bf16[6,48,256]{2,1,0:T(8,128)(2,1)S(1)} %slice.33), channel_id=1, source_target_pairs={{0,1},{1,2},{2,3},{3,0},{4,5},{5,6},{6,7},{7,4},{8,9},{9,10},{10,1... | collective-permute-start | bytes 442376 | tf_op jit(solution)/shard_map/cond/branch_1_fun/ppermute | solution.py:392
  17.8 6.7 %collective-permute-start.4 = (bf16[2,48,256]{2,1,0:T(8,128)(2,1)S(1)}, bf16[2,48,256]{2,1,0:T(8,128)(2,1)S(1)}, u32[]{:S(2)}, u32[]{:S(2)}) collective-permute-start(bf16[2,48,256]{2,1,0:T(8,128)(2,1)S(1)} %slice.32), channel_id=1, source_target_pairs={{1,0},{2,1},{3,2},{0,3},{5,4},{6,5},{7,6},{4,7},{9,8},{10,9},{11,1... | collective-permute-start | bytes 147464 | tf_op jit(solution)/shard_map/cond/branch_1_fun/ppermute | solution.py:393
  19.9 6.3 %collective-permute-start.6 = (bf16[192,256]{1,0:T(8,128)(2,1)S(1)}, bf16[192,256]{1,0:T(8,128)(2,1)S(1)}, u32[]{:S(2)}, u32[]{:S(2)}) collective-permute-start(bf16[192,256]{1,0:T(8,128)(2,1)S(1)} %get-tuple-element.92), channel_id=1, source_target_pairs={{0,4},{4,0},{1,5},{5,1},{2,6},{6,2},{3,7},{7,3},{8,12},{12,8},{9,1... | collective-permute-start | bytes 294920 | tf_op jit(solution)/shard_map/cond/branch_1_fun/ppermute | solution.py:394
  24.6 4.7 %collective-permute-start.7 = (bf16[192,256]{1,0:T(8,128)(2,1)S(1)}, bf16[192,256]{1,0:T(8,128)(2,1)S(1)}, u32[]{:S(2)}, u32[]{:S(2)}) collective-permute-start(bf16[192,256]{1,0:T(8,128)(2,1)S(1)} %get-tuple-element.100), channel_id=1, source_target_pairs={{0,4},{4,0},{1,5},{5,1},{2,6},{6,2},{3,7},{7,3},{8,12},{12,8},{9,1... | collective-permute-start | bytes 294920 | tf_op jit(solution)/shard_map/cond/branch_1_fun/ppermute | solution.py:404
